TPU v7x, 128 devices: a whole 4x4x4 slice. The times are simulated.
128 devices in a mesh: ts: 8 (over x_hi, z), dp: 2 (over x_lo), ep: 8 (over y, core).
Axes of the slice: x: 4 (x_hi: 2, x_lo: 2; x = x_hi * 2 + x_lo), y: 4, z: 4, core: 2. Of those that a mesh axis runs over, the one named last changes fastest.
Arguments:
- tokens: bfloat16 [64, 128, 2560], P(('ts', 'ep'), 'dp'), may hold values from -6 to 6
- out_grad: bfloat16 [64, 128, 2560], P(('ts', 'ep'), 'dp'), may hold values from -6 to 6
- routes: int32 [64, 128, 6], P(('ts', 'ep')), may hold values from 0 to 63, all different within a row; in each aligned block of 64 rows (0 to 63, 64 to 127, ..., all dimensions but the last counted through in order) at most 9 rows name the same one
- norm_gain: bfloat16 [2560], replicated, may hold values from 0.099609375 to 1.8984375
- router_w: bfloat16 [2560, 64], replicated, may hold values from -0.125 to 0.125
- w_gate: bfloat16 [64, 1536, 2560], P(('ts', 'ep'), 'dp'), may hold values from -0.125 to 0.125
- w_up: bfloat16 [64, 1536, 2560], P(('ts', 'ep'), 'dp'), may hold values from -0.125 to 0.125
- w_down: bfloat16 [64, 1536, 2560], P(('ts', 'ep'), 'dp'), may hold values from -0.15625 to 0.15625
Outputs:
- grad_x: float32 [64, 128, 2560], P(('ts', 'ep'), 'dp')
- grad_gate: bfloat16 [64, 1536, 2560], P(('ts', 'ep'), 'dp')
- grad_up: bfloat16 [64, 1536, 2560], P(('ts', 'ep'), 'dp')
- grad_down: bfloat16 [64, 1536, 2560], P(('ts', 'ep'), 'dp')
- grad_router: float32 [2560, 64], replicated
- grad_gain: float32 [2560], replicated
Inputs may be any that keep to these rules, and one draw needn't show every extreme that they name: `routes`: each row names 6 different experts; in the rows of one device (aligned blocks of 64 rows) no expert is named more than 9 times, a bound that some block reaches.
All inputs are finite; a program needn't handle non-finite values.
Results may differ from a plain program's by a relative error of at most 0.0079.
Values may be sent and summed in bfloat16 or wider, within the bound.
A program may use at most 192 MiB of HBM per device.

v0:
```python
from functools import partial

import jax
import jax.numpy as jnp
from jax import lax
from jax.sharding import PartitionSpec as P


def norm_parts(inputs, norm_gain):
    widened = inputs.astype(jnp.float32)
    inv_scale = lax.rsqrt(jnp.mean(widened * widened, axis=-1, keepdims=True) + 1e-06)
    normed = widened * inv_scale
    return ((normed * norm_gain.astype(jnp.float32)).astype(jnp.bfloat16), normed, inv_scale)


def block_ranks(block_routes, experts):
    flat_ids = block_routes.reshape(-1)
    onehot = (flat_ids[:, None] == jnp.arange(experts, dtype=jnp.int32)[None, :]).astype(jnp.int32)
    before = jnp.cumsum(onehot, axis=0) - onehot
    return jnp.sum(onehot * before, axis=1).reshape(block_routes.shape)


def expert_back(recv_u, recv_dy, recv_g, w_gate, w_up, w_down):
    pre_gate = jnp.einsum("secd,efd->secf", recv_u, w_gate, preferred_element_type=jnp.float32)
    pre_up = jnp.einsum("secd,efd->secf", recv_u, w_up, preferred_element_type=jnp.float32)
    active = jax.nn.silu(pre_gate)
    hidden = (active * pre_up).astype(jnp.bfloat16)
    output = jnp.einsum("secf,efd->secd", hidden, w_down, preferred_element_type=jnp.float32)
    gate_dots = jnp.sum(recv_dy.astype(jnp.float32) * output, axis=-1)
    scaled_grad = (recv_g.astype(jnp.float32)[..., None] * recv_dy.astype(jnp.float32)).astype(
        jnp.bfloat16
    )
    hidden_grad = jnp.einsum(
        "secd,efd->secf", scaled_grad, w_down, preferred_element_type=jnp.float32
    )
    sigma = jax.nn.sigmoid(pre_gate)
    gate_grad = (hidden_grad * pre_up * sigma * (1.0 + pre_gate * (1.0 - sigma))).astype(
        jnp.bfloat16
    )
    up_grad = (hidden_grad * active).astype(jnp.bfloat16)
    grad_down = jnp.einsum(
        "secf,secd->efd", hidden, scaled_grad, preferred_element_type=jnp.float32
    ).astype(jnp.bfloat16)
    grad_gate = jnp.einsum(
        "secf,secd->efd", gate_grad, recv_u, preferred_element_type=jnp.float32
    ).astype(jnp.bfloat16)
    grad_up = jnp.einsum(
        "secf,secd->efd", up_grad, recv_u, preferred_element_type=jnp.float32
    ).astype(jnp.bfloat16)
    row_grads = jnp.einsum("secf,efd->secd", gate_grad, w_gate, preferred_element_type=jnp.float32)
    row_grads = row_grads + jnp.einsum(
        "secf,efd->secd", up_grad, w_up, preferred_element_type=jnp.float32
    )
    return (row_grads, gate_dots, grad_gate, grad_up, grad_down)


def local(tokens, out_grad, routes, norm_gain, router_w, w_gate, w_up, w_down):
    tok_dev = tokens.shape[1]
    model_width = tokens.shape[2]
    top_count = routes.shape[2]
    experts = router_w.shape[1]
    exp_dev = w_gate.shape[0]
    ts_count = lax.axis_size("ts")
    share_count = lax.axis_size("dp")
    ep_count = lax.axis_size("ep")
    groups = ts_count * ep_count
    most_rows = max(2, (3 * tok_dev * top_count + 2 * experts - 1) // (2 * experts))
    own_u, own_v, own_scale = norm_parts(tokens[0], norm_gain)
    grad_out = out_grad[0]
    u_rows, dy_rows = (
        lax.all_gather(own_u, "dp", axis=0, tiled=True),
        lax.all_gather(grad_out, "dp", axis=0, tiled=True),
    )
    rows_routes = routes[0]
    blocks = rows_routes.reshape(share_count, tok_dev, top_count)
    ranks = jax.vmap(partial(block_ranks, experts=experts))(blocks).reshape(
        share_count * tok_dev, top_count
    )
    source = (jnp.arange(share_count * tok_dev, dtype=jnp.int32) // tok_dev)[:, None]
    bucket_size = share_count * most_rows
    slot_of = rows_routes * bucket_size + source * most_rows + ranks
    logits = jnp.dot(u_rows, router_w, preferred_element_type=jnp.float32)
    affinity = jax.nn.sigmoid(logits)
    picked = jnp.take_along_axis(affinity, rows_routes, axis=1)
    totals = jnp.sum(picked, axis=1, keepdims=True)
    gate_values = picked / totals
    gate_wire = gate_values.astype(jnp.bfloat16)
    slots_all = experts * bucket_size
    matches = slot_of[None, :, :] == jnp.arange(slots_all, dtype=jnp.int32)[:, None, None]
    picker = jnp.any(matches, axis=2).astype(jnp.bfloat16)
    send_u = jnp.dot(picker, u_rows, preferred_element_type=jnp.float32).astype(jnp.bfloat16)
    send_dy = jnp.dot(picker, dy_rows, preferred_element_type=jnp.float32).astype(jnp.bfloat16)
    send_g = jnp.sum(
        jnp.where(matches, gate_wire.astype(jnp.float32)[None], 0.0), axis=(1, 2)
    ).astype(jnp.bfloat16)
    recv_u, recv_dy, recv_g = (
        lax.all_to_all(
            send_u.reshape(groups, exp_dev, bucket_size, model_width),
            ("ts", "ep"),
            split_axis=0,
            concat_axis=0,
            tiled=True,
        ),
        lax.all_to_all(
            send_dy.reshape(groups, exp_dev, bucket_size, model_width),
            ("ts", "ep"),
            split_axis=0,
            concat_axis=0,
            tiled=True,
        ),
        lax.all_to_all(
            send_g.reshape(groups, exp_dev, bucket_size),
            ("ts", "ep"),
            split_axis=0,
            concat_axis=0,
            tiled=True,
        ),
    )
    row_grads, gate_dots, grad_gate, grad_up, grad_down = expert_back(
        recv_u, recv_dy, recv_g, w_gate, w_up, w_down
    )
    back_rows, back_dots = (
        lax.all_to_all(row_grads, ("ts", "ep"), split_axis=0, concat_axis=0, tiled=True),
        lax.all_to_all(gate_dots, ("ts", "ep"), split_axis=0, concat_axis=0, tiled=True),
    )
    flat_rows = back_rows.reshape(slots_all, model_width)
    flat_dots = back_dots.reshape(slots_all)
    expert_part = jnp.sum(flat_rows[slot_of], axis=1)
    pair_dots = flat_dots[slot_of]
    mixed = jnp.sum(gate_values * pair_dots, axis=1, keepdims=True)
    steer = (pair_dots - mixed) / totals
    onehot = (
        rows_routes[:, :, None] == jnp.arange(experts, dtype=jnp.int32)[None, None, :]
    ).astype(jnp.float32)
    dlogits = jnp.sum(onehot * steer[:, :, None], axis=1) * affinity * (1.0 - affinity)
    router_wide = router_w.astype(jnp.float32)
    row_grad = expert_part + jnp.dot(dlogits, router_wide.T, precision=lax.Precision.HIGHEST)
    grad_router = jnp.dot(u_rows.astype(jnp.float32).T, dlogits, precision=lax.Precision.HIGHEST)
    row_grad = lax.psum_scatter(row_grad, "dp", scatter_dimension=0, tiled=True)
    scaled = row_grad * norm_gain.astype(jnp.float32)
    grad_x = own_scale * scaled - own_v * own_scale * jnp.mean(
        own_v * scaled, axis=-1, keepdims=True
    )
    grad_gain = jnp.sum(row_grad * own_v, axis=0)
    grad_router, grad_gain = lax.psum((grad_router, grad_gain), ("ts", "dp", "ep"))
    return (grad_x[None], grad_gate, grad_up, grad_down, grad_router, grad_gain)


def solution(mesh):
    placed = (
        P(("ts", "ep"), "dp", None),
        P(("ts", "ep"), "dp", None),
        P(("ts", "ep"), None, None),
        P(),
        P(),
        P(("ts", "ep"), "dp", None),
        P(("ts", "ep"), "dp", None),
        P(("ts", "ep"), "dp", None),
    )
    return jax.shard_map(
        local,
        mesh=mesh,
        in_specs=placed,
        out_specs=(
            P(("ts", "ep"), "dp", None),
            P(("ts", "ep"), "dp", None),
            P(("ts", "ep"), "dp", None),
            P(("ts", "ep"), "dp", None),
            P(),
            P(),
        ),
        check_vma=False,
    )
```

profile of v0, /device:TPU:1, one launch (start us, length us, event | category | flops | bytes accessed | tf_op | source)
XLA Modules:
  0.0 824.8 jit_solution(17782588438587312784)
XLA Ops:
  14.9 9.6 %all_gather.6 = bf16[128,2560]{1,0:T(8,128)(2,1)S(1)} all-gather(bf16[64,2560]{1,0:T(8,128)(2,1)S(1)} %fusion.61), channel_id=1, replica_groups=mesh['ts'=8,'dp'=2,'ep'=8] {'dp'}, dimensions={0}, use_global_device_ids=true | all-gather | bytes 983040 | tf_op jit(solution)/shard_map/all_gather | solution.py:71
  24.9 5.1 gather_fusion.2
  31.9 13.0 %all-to-all-start = ((bf16[64,1,18]{2,1,0:T(2,128)(2,1)}), bf16[64,1,18]{2,1,0:T(2,128)(2,1)S(1)}, u32[]{:S(2)}, u32[]{:S(2)}) async-start(bf16[64,1,18]{2,1,0:T(2,128)(2,1)} %convert_element_type.107), calls=%async_computation | async-start | bytes 65536 | tf_op jit(solution)/shard_map/all_to_all | solution.py:111
  45.5 4.2 convolution_convert_fusion
  49.6 8.3 %reshape.277 = bf16[64,1,18,2560]{3,2,0,1:T(8,128)(2,1)} reshape(bf16[1152,2560]{1,0:T(8,128)(2,1)} %convolution_convert_fusion) | data formatting | bytes 11796480 | tf_op jit(solution)/shard_map/reshape | solution.py:98
  57.9 10.7 %all-to-all-start.2 = ((bf16[64,1,18,2560]{3,2,1,0:T(8,128)(2,1)}), bf16[64,1,18,2560]{3,2,1,0:T(8,128)(2,1)}, u32[]{:S(2)}, u32[]{:S(2)}) async-start(bf16[64,1,18,2560]{3,2,1,0:T(8,128)(2,1)} %bitcast.213), calls=%async_computation.2 | async-start | bytes 15728640 | tf_op jit(solution)/shard_map/all_to_all | solution.py:97
  68.7 101.1 %all-gather = bf16[1,128,2560]{2,1,0:T(8,128)(2,1)S(1)} all-gather(bf16[1,64,2560]{2,1,0:T(8,128)(2,1)S(1)} %copy-done.6), channel_id=2, replica_groups=mesh['ts'=8,'dp'=2,'ep'=8] {'dp'}, dimensions={1}, use_global_device_ids=true | all-gather | bytes 983040 | tf_op jit(solution)/shard_map/all_gather | solution.py:72
  173.9 8.4 %reshape.274 = bf16[64,1,18,2560]{3,2,0,1:T(8,128)(2,1)} reshape(bf16[1152,2560]{1,0:T(8,128)(2,1)} %convolution_convert_fusion.1) | data formatting | bytes 11796480 | tf_op jit(solution)/shard_map/reshape | solution.py:105
  182.2 25.8 %all-to-all-start.1 = ((bf16[64,1,18,2560]{3,2,1,0:T(8,128)(2,1)}), bf16[64,1,18,2560]{3,2,1,0:T(8,128)(2,1)}, u32[]{:S(2)}, u32[]{:S(2)}) async-start(bf16[64,1,18,2560]{3,2,1,0:T(8,128)(2,1)} %bitcast.214), calls=%async_computation.1 | async-start | bytes 15728640 | tf_op jit(solution)/shard_map/all_to_all | solution.py:104
  208.2 11.5 %fusion.7 = f32[64,18,768]{2,0,1:T(8,128)} fusion(bf16[1,768,2560]{2,1,0:T(8,128)(2,1)} %param.13, bf16[64,1,18,2560]{3,2,1,0:T(8,128)(2,1)} %all-to-all-done.2), kind=kOutput, calls=%fused_computation.18 | convolution fusion | flops 4529848320 | bytes 13369344 | tf_op jit(solution)/shard_map/secd,efd->secf/dot_general | solution.py:24
  219.7 83.3 %all-to-all-done.1 = bf16[64,1,18,2560]{3,2,1,0:T(8,128)(2,1)} async-done(((bf16[64,1,18,2560]{3,2,1,0:T(8,128)(2,1)}), bf16[64,1,18,2560]{3,2,1,0:T(8,128)(2,1)}, u32[]{:S(2)}, u32[]{:S(2)}) %all-to-all-start.1) | async-done | bytes 5898272 | tf_op jit(solution)/shard_map/all_to_all | solution.py:104
  303.0 11.8 %fusion.12 = f32[64,18,768]{2,0,1:T(8,128)} fusion(f32[64,18]{0,1:T(8,128)S(1)} %copy.122, bf16[1,768,2560]{2,1,0:T(8,128)(2,1)} %param.15, bf16[64,1,18,2560]{3,2,1,0:T(8,128)(2,1)} %all-to-all-done.1), kind=kOutput, calls=%fused_computation.22 | convolution fusion | flops 4538695680 | bytes 13373952 | tf_op jit(solution)/shard_map/secd,efd->secf/dot_general | solution.py:33
  314.8 12.5 %fusion.47 = (bf16[64,18,768]{2,0,1:T(8,128)(2,1)S(1)}, bf16[64,1,18,768]{3,0,2,1:T(8,128)(2,1)}, bf16[64,18,768]{2,0,1:T(8,128)(2,1)}) fusion(f32[64,18,768]{2,0,1:T(8,128)S(1)} %copy-done.16, f32[64,18,768]{2,0,1:T(8,128)} %fusion.12, bf16[1,768,2560]{2,1,0:T(8,128)(2,1)S(1)} %copy-done.13, bf16[64,1,18,2560]{3,2,1,0:T(8,128)(2,1)} %all-to-all-done.2), kind=kOutput, calls=%fused_computation.55 | convolution fusion | flops 4543119360 | bytes 22216704 | tf_op jit(solution)/shard_map/secd,efd->secf/dot_general | solution.py:25
  327.4 8.0 fusion.1
  336.1 19.2 %all-to-all-start.4 = ((f32[64,1,18]{2,1,0:T(1,128)}), f32[64,1,18]{2,1,0:T(1,128)S(1)}, u32[]{:S(2)}, u32[]{:S(2)}) async-start(f32[64,1,18]{2,1,0:T(1,128)} %copy.128), calls=%async_computation.4 | async-start | bytes 65536 | tf_op jit(solution)/shard_map/all_to_all | solution.py:124
  355.3 11.9 %fusion.27 = f32[64,18,2560]{2,0,1:T(8,128)} fusion(bf16[1,768,2560]{2,1,0:T(8,128)(2,1)} %param.13, bf16[64,1,18,768]{3,0,2,1:T(8,128)(2,1)} %get-tuple-element.9), kind=kOutput, calls=%fused_computation.26 | convolution fusion | flops 4529848320 | bytes 17498112 | tf_op jit(solution)/shard_map/secf,efd->secd/dot_general | solution.py:50
  367.2 7.7 add_bitcast_fusion
  374.9 13.8 %copy.127 = f32[64,1,18,2560]{3,1,2,0:T(1,128)} copy(f32[64,1,18,2560]{3,0,2,1:T(8,128)S(1)} %add_bitcast_fusion) | data formatting | bytes 23592960 | tf_op jit(solution)/shard_map/add | solution.py:51
  388.7 10.6 %all-to-all-start.3 = ((f32[64,1,18,2560]{3,1,2,0:T(1,128)}), f32[64,1,18,2560]{3,1,2,0:T(1,128)}, u32[]{:S(2)}, u32[]{:S(2)}) async-start(f32[64,1,18,2560]{3,1,2,0:T(1,128)} %copy.127), calls=%async_computation.3 | async-start | bytes 23592960 | tf_op jit(solution)/shard_map/all_to_all | solution.py:123
  399.5 10.2 %fusion.18 = bf16[1,768,2560]{2,1,0:T(8,128)(2,1)} fusion(bf16[64,1,18,768]{3,0,2,1:T(8,128)(2,1)} %get-tuple-element.9, bf16[64,1,18,2560]{3,2,1,0:T(8,128)(2,1)} %all-to-all-done.2), kind=kOutput, calls=%fused_computation.23 | convolution fusion | flops 4531814400 | bytes 11599872 | tf_op jit(solution)/shard_map/secf,secd->efd/dot_general | solution.py:44
  411.1 4.5 gather_fusion.1
  415.8 134.0 %all-to-all-done.3 = f32[64,1,18,2560]{3,1,2,0:T(1,128)} async-done(((f32[64,1,18,2560]{3,1,2,0:T(1,128)}), f32[64,1,18,2560]{3,1,2,0:T(1,128)}, u32[]{:S(2)}, u32[]{:S(2)}) %all-to-all-start.3) | async-done | bytes 11796512 | tf_op jit(solution)/shard_map/all_to_all | solution.py:123
  549.8 35.5 %reduce.2 = f32[64,18,2560]{2,1,0:T(8,128)} reduce(f32[64,1,18,2560]{3,1,2,0:T(1,128)} %all-to-all-done.3, f32[]{:T(128)} %constant.79), dimensions={1}, to_apply=%all_to_all.18.reduce_sub_computation | reduce | bytes 23592964 | tf_op jit(solution)/shard_map/all_to_all | solution.py:123
  585.3 12.0 %reshape.283 = f32[1152,2560]{1,0:T(8,128)} reshape(f32[64,18,2560]{2,1,0:T(8,128)} %reduce.2) | data formatting | bytes 23592960 | tf_op jit(solution)/shard_map/reshape | solution.py:126
  597.4 12.8 %gather_fusion = f32[768,2560]{1,0:T(8,128)} fusion(f32[1152,2560]{1,0:T(8,128)} %reshape.283, s32[1024]{0:T(1024)S(1)} %pad_clamp_fusion), kind=kCustom, calls=%fused_computation | custom fusion | bytes 15731712 | tf_op jit(solution)/shard_map/gather | solution.py:128
  610.1 9.4 %reshape.295 = f32[128,6,2560]{2,1,0:T(8,128)} reshape(f32[768,2560]{1,0:T(8,128)} %gather_fusion) | data formatting | bytes 15728640 | tf_op jit(solution)/shard_map/gather | solution.py:128
  619.6 7.2 reduce_sum.96
  628.6 9.8 %fusion.21 = bf16[1,768,2560]{2,1,0:T(8,128)(2,1)} fusion(bf16[64,18,768]{2,0,1:T(8,128)(2,1)} %get-tuple-element.10, bf16[64,1,18,2560]{3,2,1,0:T(8,128)(2,1)} %all-to-all-done.2), kind=kOutput, calls=%fused_computation.24 | convolution fusion | flops 4531814400 | bytes 11599872 | tf_op jit(solution)/shard_map/secf,secd->efd/dot_general | solution.py:47
  638.4 12.2 %fusion.24 = bf16[1,768,2560]{2,1,0:T(8,128)(2,1)} fusion(bf16[64,18,768]{2,0,1:T(8,128)(2,1)S(1)} %get-tuple-element.8, f32[64,18]{0,1:T(8,128)S(1)} %copy.122, bf16[64,1,18,2560]{3,2,1,0:T(8,128)(2,1)} %all-to-all-done.1), kind=kOutput, calls=%fused_computation.25 | convolution fusion | flops 4540661760 | bytes 11604480 | tf_op jit(solution)/shard_map/secf,secd->efd/dot_general | solution.py:41
  651.8 20.4 %reduce-scatter.2.cloned.1.call-done = f32[64,2560]{1,0:T(8,128)} async-done(((f32[128,2560]{1,0:T(8,128)}), f32[64,2560]{1,0:T(8,128)}) %reduce-scatter.2.cloned.1.call-update) | async-done | bytes 655376 | tf_op jit(solution)/shard_map/reduce_scatter | solution.py:139
  675.8 66.5 %psum.15 = f32[2560]{0:T(1024)} all-reduce(f32[2560]{0:T(1024)S(1)} %get-tuple-element.6), channel_id=1, replica_groups=mesh['ts'=8,'dp'=2,'ep'=8] {'ts','dp','ep'}, use_global_device_ids=true, to_apply=%region_15.16 | all-reduce | flops 2560 | bytes 20480 | tf_op jit(solution)/shard_map/psum | solution.py:145
  742.3 72.8 %all-reduce.2.cloned.1.call-done = f32[2560,64]{0,1:T(8,128)} async-done(((f32[2560,64]{0,1:T(8,128)}), f32[2560,64]{0,1:T(8,128)}) %all-reduce.2.cloned.1.call-update) | async-done | bytes 655376 | tf_op jit(solution)/shard_map/psum | solution.py:145
  (96 shorter events, 25.0 us)
Async XLA Ops:
  8.0 16.5 %copy-start = (bf16[2560,64]{0,1:T(8,128)(2,1)S(1)}, bf16[2560,64]{0,1:T(8,128)(2,1)}, u32[]{:S(2)}) copy-start(bf16[2560,64]{0,1:T(8,128)(2,1)} %param.12) | copy-start | bytes 983044
  12.8 2.1 copy-start.10
  13.5 1.4 copy-start.7
  24.5 20.9 %copy-start.3 = (bf16[128,2560]{1,0:T(8,128)(2,1)}, bf16[128,2560]{1,0:T(8,128)(2,1)S(1)}, u32[]{:S(2)}) copy-start(bf16[128,2560]{1,0:T(8,128)(2,1)S(1)} %all_gather.6) | copy-start | bytes 1966084
  24.9 5.1 copy-start.1
  24.9 5.5 copy-start.9
  31.9 26.1 %all-to-all-start = ((bf16[64,1,18]{2,1,0:T(2,128)(2,1)}), bf16[64,1,18]{2,1,0:T(2,128)(2,1)S(1)}, u32[]{:S(2)}, u32[]{:S(2)}) async-start(bf16[64,1,18]{2,1,0:T(2,128)(2,1)} %convert_element_type.107), calls=%async_computation | async-start | bytes 65536 | tf_op jit(solution)/shard_map/all_to_all | solution.py:111
  57.9 10.7 %copy-start.6 = (bf16[1,64,2560]{2,1,0:T(8,128)(2,1)S(1)}, bf16[1,64,2560]{2,1,0:T(8,128)(2,1)}, u32[]{:S(2)}) copy-start(bf16[1,64,2560]{2,1,0:T(8,128)(2,1)} %param.9) | copy-start | bytes 983044
  57.9 124.3 %all-to-all-start.2 = ((bf16[64,1,18,2560]{3,2,1,0:T(8,128)(2,1)}), bf16[64,1,18,2560]{3,2,1,0:T(8,128)(2,1)}, u32[]{:S(2)}, u32[]{:S(2)}) async-start(bf16[64,1,18,2560]{3,2,1,0:T(8,128)(2,1)} %bitcast.213), calls=%async_computation.2 | async-start | bytes 15728640 | tf_op jit(solution)/shard_map/all_to_all | solution.py:97
  182.2 120.7 %all-to-all-start.1 = ((bf16[64,1,18,2560]{3,2,1,0:T(8,128)(2,1)}), bf16[64,1,18,2560]{3,2,1,0:T(8,128)(2,1)}, u32[]{:S(2)}, u32[]{:S(2)}) async-start(bf16[64,1,18,2560]{3,2,1,0:T(8,128)(2,1)} %bitcast.214), calls=%async_computation.1 | async-start | bytes 15728640 | tf_op jit(solution)/shard_map/all_to_all | solution.py:104
  303.0 11.8 %copy-start.13 = (bf16[1,768,2560]{2,1,0:T(8,128)(2,1)S(1)}, bf16[1,768,2560]{2,1,0:T(8,128)(2,1)}, u32[]{:S(2)}) copy-start(bf16[1,768,2560]{2,1,0:T(8,128)(2,1)} %param.14) | copy-start | bytes 11796484
  303.0 11.8 %copy-start.16 = (f32[64,18,768]{2,0,1:T(8,128)S(1)}, f32[64,18,768]{2,0,1:T(8,128)}, u32[]{:S(2)}) copy-start(f32[64,18,768]{2,0,1:T(8,128)} %fusion.7) | copy-start | bytes 10616836
  314.8 12.5 %copy-start.12 = (bf16[1,768,2560]{2,1,0:T(8,128)(2,1)S(1)}, bf16[1,768,2560]{2,1,0:T(8,128)(2,1)}, u32[]{:S(2)}) copy-start(bf16[1,768,2560]{2,1,0:T(8,128)(2,1)} %param.15) | copy-start | bytes 11796484
  336.1 52.6 %all-to-all-start.4 = ((f32[64,1,18]{2,1,0:T(1,128)}), f32[64,1,18]{2,1,0:T(1,128)S(1)}, u32[]{:S(2)}, u32[]{:S(2)}) async-start(f32[64,1,18]{2,1,0:T(1,128)} %copy.128), calls=%async_computation.4 | async-start | bytes 65536 | tf_op jit(solution)/shard_map/all_to_all | solution.py:124
  355.2 11.9 %copy-start.14 = (bf16[1,768,2560]{2,1,0:T(8,128)(2,1)S(1)}, bf16[1,768,2560]{2,1,0:T(8,128)(2,1)}, u32[]{:S(2)}) copy-start(bf16[1,768,2560]{2,1,0:T(8,128)(2,1)} %param.14) | copy-start | bytes 11796484
  355.3 11.9 %copy-start.15 = (bf16[64,18,768]{2,0,1:T(8,128)(2,1)S(1)}, bf16[64,18,768]{2,0,1:T(8,128)(2,1)}, u32[]{:S(2)}) copy-start(bf16[64,18,768]{2,0,1:T(8,128)(2,1)} %get-tuple-element.10) | copy-start | bytes 5308420
  388.7 161.1 %all-to-all-start.3 = ((f32[64,1,18,2560]{3,1,2,0:T(1,128)}), f32[64,1,18,2560]{3,1,2,0:T(1,128)}, u32[]{:S(2)}, u32[]{:S(2)}) async-start(f32[64,1,18,2560]{3,1,2,0:T(1,128)} %copy.127), calls=%async_computation.3 | async-start | bytes 23592960 | tf_op jit(solution)/shard_map/all_to_all | solution.py:123
  399.3 272.9 %reduce-scatter.2.cloned.1.call-start = ((), (), s32[]{:S(2)}) async-start(), calls=%async_computation.6 | async-start | bytes 1966080 | tf_op jit(solution)/shard_map/reduce_scatter | solution.py:139
  619.6 7.2 copy-start.2
  628.6 186.6 %all-reduce.2.cloned.1.call-start = ((), (), s32[]{:S(2)}) async-start(), calls=%async_computation.7 | async-start | bytes 1310720 | tf_op jit(solution)/shard_map/psum | solution.py:145
  638.4 12.2 %copy-start.4 = (bf16[128,2560]{1,0:T(8,128)(2,1)S(1)}, bf16[128,2560]{1,0:T(8,128)(2,1)}, u32[]{:S(2)}) copy-start(bf16[128,2560]{1,0:T(8,128)(2,1)} %copy-done.3) | copy-start | bytes 1966084
  638.4 33.9 %copy-start.5 = (bf16[1,64,2560]{2,1,0:T(8,128)(2,1)S(1)}, bf16[1,64,2560]{2,1,0:T(8,128)(2,1)}, u32[]{:S(2)}) copy-start(bf16[1,64,2560]{2,1,0:T(8,128)(2,1)} %param.8) | copy-start | bytes 983044
  638.4 33.9 %copy-start.8 = (f32[2560]{0:T(1024)S(1)}, f32[2560]{0:T(1024)}, u32[]{:S(2)}) copy-start(f32[2560]{0:T(1024)} %copy-done.7) | copy-start | bytes 30724
  638.4 33.9 %copy-start.11 = (f32[64]{0:T(128)S(1)}, f32[64]{0:T(128)}, u32[]{:S(2)}) copy-start(f32[64]{0:T(128)} %copy-done.10) | copy-start | bytes 772
Sparse Core Ops, SparseCore 0:
  628.7 43.5 reduce-scatter.1
Sparse Core Ops, SparseCore 1:
  651.9 163.2 all-reduce.1
where the time goes:
time: 833 us; the launch traced here: 825 us
  waiting for transfers between devices  311 us (37%)
  blocking collectives  177 us (21%)
  matrix products  107 us (13%)
  local copies, waits for them, and re-layouts  81.1 us (10%)
  starting transfers between devices  79.3 us (10%)
  other arithmetic  53.2 us (6%)
  between operations  16.1 us (2%)
    all_to_all x1, waiting for transfers between devices, local(): lax.all_to_all(row_grads, ('ts', 'ep'), split_axis=0, concat_axis=0, tile...  134 us
    all_gather x1, blocking collectives, local(): lax.all_gather(grad_out, 'dp', axis=0, tiled=True)  101 us
    all_to_all x1, waiting for transfers between devices, local(): lax.all_to_all(send_dy.reshape(groups, exp_dev, bucket_size, model_width)...  83.3 us
    psum x1, waiting for transfers between devices, local(): lax.psum((grad_router, grad_gain), ('ts', 'dp', 'ep'))  72.8 us
    psum x1, blocking collectives, local(): lax.psum((grad_router, grad_gain), ('ts', 'dp', 'ep'))  66.5 us
    all_to_all x1, other arithmetic, local(): lax.all_to_all(row_grads, ('ts', 'ep'), split_axis=0, concat_axis=0, tile...  35.5 us
    all_to_all x1, starting transfers between devices, local(): lax.all_to_all(send_dy.reshape(groups, exp_dev, bucket_size, model_width)...  25.8 us
    gather x2, local copies, waits for them, and re-layouts, local(): expert_part = jnp.sum(flat_rows[slot_of], axis=1)  22.2 us
  transfers between devices with their start and end apart: 7, of which 4 were waited for; matrix products, arithmetic and copies ran while one was open for 14% of the time, Pallas kernels for 0%

commit v1 on v0

v1 whole, which is shorter than its diff:
```python
import jax
import jax.numpy as jnp
from jax import lax
from jax.experimental import pallas as pl
from jax.experimental.pallas import tpu as pltpu
from jax.sharding import PartitionSpec as P

MESH = pl.DeviceIdType.MESH
F32 = jnp.float32
BF16 = jnp.bfloat16
D = 2560
NC = 4
CW = D // NC
TOK = 64
MOST = 9
SRC = 16
MSG = SRC * MOST
PEERS = 8
ROWS = PEERS * MSG
ALL = SRC * TOK
SH = 768
EXPERTS = 64
KA = 640
KB = ROWS - KA
NT = (((1,), (1,)), ((), ()))
TN = (((0,), (0,)), ((), ()))


def dot(a, b, dims=(((1,), (0,)), ((), ()))):
    return lax.dot_general(a, b, dims, preferred_element_type=F32)


def split(a):
    hi = a.astype(BF16)
    return hi, (a - hi.astype(F32)).astype(BF16)


def kernel(
    tok, dy, rt, gain, rwt, wg_in, wu_in, wd_in,
    gx_out, gr_out, gn_out, gg_out, gu_out, gd_out,
    xall, rall, send, wg, wu, wd, acc1, acc2, q, s, h, da, db, pk,
    rts, zt, slots, gs, gr, ds_, dr, dgt, dgr, gwrow, dgrow, rowg, dzs, gaccum,
    wsem, osem, lsem,
    rt_ss, rt_rs, a_ss, a_rs, b_ss, b_rs, d_ss, d_rs, g_ss, g_rs, dg_ss, dg_rs, dt_ss, dt_rs,
    r_ss, r_rs, z_ss, z_rs, x_ss, x_rs, free_sem,
):
    ts, dp, ep = lax.axis_index("ts"), lax.axis_index("dp"), lax.axis_index("ep")
    xh, z = ts // 4, ts % 4
    x = xh * 2 + dp
    y, core = ep // 2, ep % 2
    me = z * 4 + x

    def at_xz(zz, xx):
        return ((xx // 2) * 4 + zz, xx % 2, ep)

    def at_ep(e):
        return (ts, dp, e)

    def remote(src, dst, ss, rs, dev):
        return pltpu.make_async_remote_copy(
            src_ref=src, dst_ref=dst, send_sem=ss, recv_sem=rs, device_id=dev, device_id_type=MESH
        )

    def wcopy(i, c):
        src, dst = ((wg_in, wg), (wu_in, wu), (wd_in, wd))[i]
        return pltpu.make_async_copy(src.at[:, pl.ds(c * CW, CW)], dst.at[c], wsem.at[i, c])

    for c in range(NC):
        for i in range(3):
            wcopy(i, c).start()

    barrier = pltpu.get_barrier_semaphore()
    for i in range(1, PEERS):
        pl.semaphore_signal(barrier, inc=1, device_id=at_ep((ep + i) % PEERS), device_id_type=MESH)
    for i in range(1, SRC):
        p = (me + i) % SRC
        pl.semaphore_signal(barrier, inc=1, device_id=at_xz(p // 4, p % 4), device_id_type=MESH)
    pl.semaphore_wait(barrier, PEERS - 1 + SRC - 1)

    myb = z * 2 + xh
    rts[myb] = rt[...]

    def rt_copy(i):
        t = (ts + i) % 8
        return remote(rt, rts.at[myb], rt_ss.at[i - 1], rt_rs.at[i - 1], (t, dp, ep))

    for i in range(1, 8):
        rt_copy(i).start()

    mine = pl.multiple_of(me * TOK, TOK)
    wide = tok[...].astype(F32)
    inv = lax.rsqrt(jnp.mean(wide * wide, axis=1, keepdims=True) + 1e-06)
    u_own = (wide * inv * gain[...]).astype(BF16)
    for c in range(NC):
        xall[c, pl.ds(mine, TOK), :] = u_own[:, c * CW : (c + 1) * CW]
        xall[NC + c, pl.ds(mine, TOK), :] = dy[:, c * CW : (c + 1) * CW]

    def a_copy(st, i):
        block = xall.at[st, pl.ds(mine, TOK)]
        return remote(block, block, a_ss.at[st, i - 1], a_rs.at[st, i - 1], at_xz(z, (x + i) % 4))

    line = pl.multiple_of(z * 4 * TOK, 4 * TOK)

    def b_copy(st, i):
        block = xall.at[st, pl.ds(line, 4 * TOK)]
        return remote(block, block, b_ss.at[st, i - 1], b_rs.at[st, i - 1], at_xz((z + i) % 4, x))

    for st in range(2 * NC):
        for i in (1, 3, 2):
            a_copy(st, i).start()

    def forward(st):
        for i in (1, 3, 2):
            a_copy(st, i).wait_recv()
        for i in (1, 3, 2):
            b_copy(st, i).start()

    forward(0)
    forward(1)

    for i in range(1, 8):
        rt_copy(i).wait_recv()
    lane = lax.broadcasted_iota(jnp.int32, (128, 128), 1)
    sub = lax.broadcasted_iota(jnp.int32, (128, 128), 0)
    before = jnp.where((sub < lane) & ((sub // TOK) == (lane // TOK)), 1.0, 0.0).astype(BF16)
    for b in range(8):
        r = rts[b]
        ids = lax.broadcasted_iota(jnp.int32, (16, 128), 0)
        own = jnp.zeros((16, 128), F32)
        for k in range(6):
            own = own + jnp.where((r[k : k + 1, :] == ts * PEERS + ids) & (ids < PEERS), 1.0, 0.0)
        rank = dot(own.astype(BF16), before)
        half = lax.broadcasted_iota(jnp.int32, (16, 128), 1) // TOK
        slot = jnp.where(own > 0.5, (2 * b + half) * MOST + rank.astype(jnp.int32), -1)
        slots[:, b * 128 : (b + 1) * 128] = slot

    def slot_body(d, _):
        row = slots[pl.ds(d, 1), :]
        hit = lax.broadcasted_iota(jnp.int32, (MSG, ALL), 0) == row
        pk[pl.ds(pl.multiple_of(d * MSG, MSG), MSG), :] = jnp.where(hit, 1.0, 0.0).astype(BF16)
        return 0

    lax.fori_loop(0, PEERS, slot_body, 0)
    def d_copy(st, i):
        e = (ep + i) % PEERS
        return remote(
            send.at[st % NC, pl.ds(pl.multiple_of(e * MSG, MSG), MSG)],
            rall.at[st, pl.ds(pl.multiple_of(ep * MSG, MSG), MSG)],
            d_ss.at[st, i - 1],
            d_rs.at[st, i - 1],
            at_ep(e),
        )

    own_rows = pl.ds(pl.multiple_of(ep * MSG, MSG), MSG)

    def own_copy(st):
        return pltpu.make_async_copy(send.at[st % NC, own_rows], rall.at[st, own_rows], lsem.at[st])

    def pack(st):
        for i in (1, 3, 2):
            b_copy(st, i).wait_recv()

        def body(i, _):
            yy = (y + 1 + i) % 4
            rows = pl.ds(pl.multiple_of(yy * 2 * MSG, 2 * MSG), 2 * MSG)
            send[st % NC, rows, :] = dot(pk[rows, :], xall[st, pl.ds(0, ALL), :]).astype(BF16)
            for cc in range(2):
                e = yy * 2 + cc

                @pl.when(e != ep)
                def _():
                    d_copy(st, (e - ep + PEERS) % PEERS).start()

            return 0

        lax.fori_loop(0, 4, body, 0)
        own_copy(st).start()

    def u_body(c, _):
        @pl.when(c + 2 < 2 * NC)
        def _():
            forward(c + 2)

        pack(c)
        part = dot(rwt[c], xall[c, pl.ds(0, ALL), :], NT)

        @pl.when(c == 0)
        def _():
            zt[...] = part

        @pl.when(c > 0)
        def _():
            zt[...] += part

        return 0

    lax.fori_loop(0, NC, u_body, 0)

    for b in range(8):
        lanes = slice(b * 128, (b + 1) * 128)
        r = rts[b]
        ids = lax.broadcasted_iota(jnp.int32, (EXPERTS, 128), 0)
        mask = jnp.zeros((EXPERTS, 128), F32)
        for k in range(6):
            mask = mask + jnp.where(r[k : k + 1, :] == ids, 1.0, 0.0)
        sg = jax.nn.sigmoid(zt[:, lanes])
        zt[:, lanes] = sg
        rowg[:, lanes] = jnp.sum(mask * sg, axis=0, keepdims=True)
    gt = (zt[pl.ds(pl.multiple_of(ts * PEERS, PEERS), PEERS), :] / rowg[...]).astype(BF16)

    def g_copy(i):
        e = (ep + i) % PEERS
        return remote(gs.at[e], gr.at[ep], g_ss.at[i - 1], g_rs.at[i - 1], at_ep(e))

    for d in range(PEERS):
        gs[d, :, 0:MSG] = dot(gt, pk[d * MSG : (d + 1) * MSG, :], NT)[d : d + 1, :] + jnp.zeros((8, MSG), F32)
        gs[d, :, MSG:256] = jnp.zeros((8, 256 - MSG), F32)
    gr[ep] = gs[ep]
    for i in range(1, PEERS):
        g_copy(i).start()

    def wait_d(st):
        for i in range(1, PEERS):
            d_copy(st, i).wait_recv()
        own_copy(st).wait()

    NTILE = ROWS // 3

    def ab_body(c, _):
        for i in range(1, PEERS):
            d_copy(c, i).wait_send()

        @pl.when(c + 2 < NC)
        def _():
            forward(NC + c + 2)

        wait_d(c)
        for i in (1, 3, 2):
            a_copy(c, i).wait_send()
            b_copy(c, i).wait_send()
        pack(NC + c)
        for i in range(2):
            wcopy_dyn(i, c).wait()

        def tile(t, _):
            cols = pl.ds(pl.multiple_of(t * NTILE, NTILE), NTILE)
            rows = rall[c, cols, :]
            pa = dot(wg[c], rows, NT)
            pb = dot(wu[c], rows, NT)

            @pl.when(c == 0)
            def _():
                acc1[:, cols] = pa
                acc2[:, cols] = pb

            @pl.when(c > 0)
            def _():
                acc1[:, cols] += pa
                acc2[:, cols] += pb

            return 0

        lax.fori_loop(0, 3, tile, 0)
        return 0

    def wcopy_dyn(i, c):
        src, dst = ((wg_in, wg), (wu_in, wu), (wd_in, wd))[i]
        return pltpu.make_async_copy(
            src.at[:, pl.ds(pl.multiple_of(c * CW, CW), CW)], dst.at[c], wsem.at[i, c]
        )

    lax.fori_loop(0, NC, ab_body, 0)

    def drain(st, _):
        for i in (1, 3, 2):
            a_copy(st, i).wait_send()
            b_copy(st, i).wait_send()
        return 0

    lax.fori_loop(NC, 2 * NC, drain, 0)
    for i in range(1, 4):
        pl.semaphore_signal(free_sem, inc=1, device_id=at_xz((z + i) % 4, x), device_id_type=MESH)
        pl.semaphore_signal(free_sem, inc=1, device_id=at_xz(z, (x + i) % 4), device_id_type=MESH)

    FT = 32

    def act_body(t, _):
        f = pl.ds(pl.multiple_of(t * FT, FT), FT)
        a, b = acc1[f, :], acc2[f, :]
        sg = jax.nn.sigmoid(a)
        act = a * sg
        h[f, :] = (act * b).astype(BF16)
        s[f, :] = act.astype(BF16)
        q[f, :] = (b * sg * (1.0 + a * (1.0 - sg))).astype(BF16)
        return 0

    lax.fori_loop(0, SH // FT, act_body, 0)

    for i in range(1, PEERS):
        g_copy(i).wait_recv()
    total = jnp.zeros((8, ROWS + 128), F32)
    zpad = jnp.zeros((8, ROWS + 128 - 256), F32)
    for e in range(PEERS):
        piece = jnp.concatenate([gr[e], zpad], axis=1)
        total = total + (pltpu.roll(piece, e * MSG, 1) if e else piece)
    gwrow[...] = total[:, 0:ROWS]

    def p_body(c, _):
        wait_d(NC + c)
        wcopy_dyn(2, c).wait()

        def tile(t, _):
            cols = pl.ds(pl.multiple_of(t * NTILE, NTILE), NTILE)
            pp = dot(wd[c], rall[NC + c, cols, :], NT)

            @pl.when(c == 0)
            def _():
                acc1[:, cols] = pp

            @pl.when(c > 0)
            def _():
                acc1[:, cols] += pp

            return 0

        lax.fori_loop(0, 3, tile, 0)
        return 0

    lax.fori_loop(0, NC, p_body, 0)

    dgrow[...] = jnp.zeros_like(dgrow)
    GT = 128

    def grad_body(t, _):
        f = pl.ds(pl.multiple_of(t * GT, GT), GT)
        part = jnp.zeros((8, ROWS), F32)
        gw = gwrow[0:1, :]
        for k in range(GT // 16):
            fk = pl.ds(pl.multiple_of(t * GT + k * 16, 16), 16)
            p = acc1[fk, :]
            hh = h[fk, :].astype(F32)
            prod = hh * p
            part = part + prod[0:8] + prod[8:16]
            dh = p * gw
            q[fk, :] = (dh * q[fk, :].astype(F32)).astype(BF16)
            s[fk, :] = (dh * s[fk, :].astype(F32)).astype(BF16)
            h[fk, :] = (hh * gw).astype(BF16)
        dgrow[...] += part
        da[:, f] = jnp.transpose(q[f, :])
        db[:, f] = jnp.transpose(s[f, :])
        return 0

    lax.fori_loop(0, SH // GT, grad_body, 0)

    def dg_copy(i):
        e = (ep + i) % PEERS
        return remote(ds_.at[e], dr.at[ep], dg_ss.at[i - 1], dg_rs.at[i - 1], at_ep(e))

    dg = jnp.sum(dgrow[...], axis=0, keepdims=True) + jnp.zeros((8, ROWS), F32)
    dg = jnp.concatenate([dg, jnp.zeros((8, 128), F32)], axis=1)
    keep = lax.broadcasted_iota(jnp.int32, (8, 256), 1) < MSG
    for e in range(PEERS):
        moved = pltpu.roll(dg, ROWS + 128 - e * MSG, 1) if e else dg
        ds_[e] = jnp.where(keep, moved[:, 0:256], 0.0)
    dr[ep] = ds_[ep]
    for i in range(1, PEERS):
        dg_copy(i).start()

    def ret_copy(c, i):
        e = (ep + i) % PEERS
        return remote(
            send.at[c, pl.ds(pl.multiple_of(e * MSG, MSG), MSG)],
            xall.at[c, own_rows],
            r_ss.at[c, i - 1],
            r_rs.at[c, i - 1],
            at_ep(e),
        )

    def own_ret(c):
        return pltpu.make_async_copy(send.at[c, own_rows], xall.at[c, own_rows], lsem.at[c])

    def ret_body(c, _):
        for i in range(1, PEERS):
            d_copy(NC + c, i).wait_send()

        def body(i, _):
            yy = (y + 1 + i) % 4
            rows = pl.ds(pl.multiple_of(yy * 2 * MSG, 2 * MSG), 2 * MSG)
            send[c, rows, :] = (dot(da[rows, :], wg[c]) + dot(db[rows, :], wu[c])).astype(BF16)
            for cc in range(2):
                e = yy * 2 + cc

                @pl.when(e != ep)
                def _():
                    ret_copy(c, (e - ep + PEERS) % PEERS).start()

            return 0

        lax.fori_loop(0, 4, body, 0)
        own_ret(c).start()
        return 0

    lax.fori_loop(0, NC, ret_body, 0)

    for b in range(8):
        lanes = slice(b * 128, (b + 1) * 128)
        da[lanes, 0:KA] = jnp.transpose(pk[0:KA, lanes])
        db[lanes, 0:KB] = jnp.transpose(pk[KA:ROWS, lanes])

    def out_copy(i, c):
        src, dst = ((wg, gg_out), (wu, gu_out), (wd, gd_out))[i]
        return pltpu.make_async_copy(
            src.at[c], dst.at[:, pl.ds(pl.multiple_of(c * CW, CW), CW)], osem.at[i, c]
        )

    MT = 256

    def wgrad_body(c, _):
        gaccum[c] = jnp.zeros((8, CW), F32)

        def tile(t, _):
            f = pl.ds(pl.multiple_of(t * MT, MT), MT)
            ga = dot(q[f, :], rall[c])
            part = jnp.sum(ga * wg[c, f, :].astype(F32), axis=0, keepdims=True)
            wg[c, f, :] = ga.astype(BF16)
            gb = dot(s[f, :], rall[c])
            part = part + jnp.sum(gb * wu[c, f, :].astype(F32), axis=0, keepdims=True)
            wu[c, f, :] = gb.astype(BF16)
            gaccum[c] += part + jnp.zeros((8, CW), F32)
            wd[c, f, :] = dot(h[f, :], rall[NC + c]).astype(BF16)
            return 0

        lax.fori_loop(0, SH // MT, tile, 0)
        for i in range(3):
            out_copy(i, c).start()
        return 0

    lax.fori_loop(0, NC, wgrad_body, 0)
    for c in range(NC):
        gn_out[:, c * CW : (c + 1) * CW] = gaccum[c]

    def dt_copy(i):
        p = (me + i) % SRC
        zz, xx = p // 4, p % 4
        return remote(dgt.at[zz * 2 + xx // 2], dgr.at[me], dt_ss.at[i - 1], dt_rs.at[i - 1], at_xz(zz, xx))

    for i in range(1, PEERS):
        dg_copy(i).wait_recv()
    for d in range(PEERS):
        hi, lo = split(dr[d][:, 0:MSG])
        rows = pk[d * MSG : (d + 1) * MSG, :]
        got = dot(hi, rows) + dot(lo, rows)
        for b in range(8):
            dgt[b, d : d + 1, :] = got[0:1, b * 128 : (b + 1) * 128]
    dgr[me] = dgt[myb]
    for i in range(1, SRC):
        dt_copy(i).start()

    pl.semaphore_wait(free_sem, 6)

    def z_copy(c, i):
        zz = (z + i) % 4
        return remote(
            send.at[c, pl.ds(pl.multiple_of(zz * 4 * TOK, 4 * TOK), 4 * TOK)],
            xall.at[NC + c, pl.ds((i - 1) * 4 * TOK, 4 * TOK)],
            z_ss.at[c, i - 1],
            z_rs.at[c, i - 1],
            at_xz(zz, x),
        )

    def x_copy(c, i):
        xx = (x + i) % 4
        return remote(
            send.at[c, pl.ds(pl.multiple_of(line + xx * TOK, TOK), TOK)],
            xall.at[NC + c, pl.ds(12 * TOK + (i - 1) * TOK, TOK)],
            x_ss.at[c, i - 1],
            x_rs.at[c, i - 1],
            at_xz(z, xx),
        )

    def comb_body(c, _):
        for i in range(1, PEERS):
            ret_copy(c, i).wait_recv()
            ret_copy(c, i).wait_send()
        own_ret(c).wait()

        def body(i, _):
            zz = (z + 1 + i) % 4
            rows = pl.ds(pl.multiple_of(zz * 4 * TOK, 4 * TOK), 4 * TOK)
            low = dot(da[rows, 0:KA], xall[c, 0:KA, :])
            send[c, rows, :] = (low + dot(db[rows, 0:KB], xall[c, KA:ROWS, :])).astype(BF16)

            @pl.when(i < 3)
            def _():
                z_copy(c, i + 1).start()

            return 0

        lax.fori_loop(0, 4, body, 0)
        return 0

    def z_sum(c):
        for i in (1, 3, 2):
            z_copy(c, i).wait_recv()
        rows = pl.ds(line, 4 * TOK)
        tot = send[c, rows, :].astype(F32)
        for i in range(3):
            tot = tot + xall[NC + c, i * 4 * TOK : (i + 1) * 4 * TOK, :].astype(F32)
        send[c, rows, :] = tot.astype(BF16)
        for i in (1, 3, 2):
            x_copy(c, i).start()

    def comb_loop(c, _):
        comb_body(c, 0)

        @pl.when(c > 0)
        def _():
            z_sum(c - 1)

        return 0

    lax.fori_loop(0, NC, comb_loop, 0)
    z_sum(NC - 1)

    for i in range(1, SRC):
        dt_copy(i).wait_recv()
    for t in range(8):
        zz, hh = t % 4, t // 4
        j = zz * 4 + hh * 2
        dzs[t * 8 : (t + 1) * 8, :] = dgr[j] + dgr[j + 1]
    lanes = pl.ds(pl.multiple_of(myb * 128, 128), 128)
    r = rt[...]
    ids = lax.broadcasted_iota(jnp.int32, (EXPERTS, 128), 0)
    mask = jnp.zeros((EXPERTS, 128), F32)
    for k in range(6):
        mask = mask + jnp.where(r[k : k + 1, :] == ids, 1.0, 0.0)
    sg = zt[:, lanes]
    tot = rowg[0:1, lanes]
    dg = dzs[...]
    mixed = jnp.sum(mask * (sg / tot) * dg, axis=0, keepdims=True)
    dz = mask * ((dg - mixed) / tot) * sg * (1.0 - sg)
    pad = jnp.concatenate([dz, jnp.zeros((64, 128), F32)], axis=0)
    dzs2 = jnp.transpose(pad)
    acc1[0:128, 0:128] = dzs2
    dz_own = acc1[pl.ds(pl.multiple_of(dp * TOK, TOK), TOK), 0:EXPERTS]
    hi, lo = split(dz_own)
    wide = tok[...].astype(F32)
    inv = lax.rsqrt(jnp.mean(wide * wide, axis=1, keepdims=True) + 1e-06)
    u_own = (wide * inv * gain[...]).astype(BF16)
    gr_out[...] = dot(hi, u_own, TN) + dot(lo, u_own, TN)

    for c in range(NC):
        cols = slice(c * CW, (c + 1) * CW)
        du = dot(hi, rwt[c]) + dot(lo, rwt[c])
        for i in (1, 3, 2):
            x_copy(c, i).wait_recv()
        du = du + send[c, pl.ds(mine, TOK), :].astype(F32)
        for i in range(3):
            du = du + xall[NC + c, (12 + i) * TOK : (13 + i) * TOK, :].astype(F32)
        gx_out[:, cols] = du * gain[:, cols]
    v = wide * inv
    scaled = gx_out[...]
    gx_out[...] = inv * scaled - v * inv * jnp.mean(v * scaled, axis=1, keepdims=True)

    def drain2(c, _):
        for i in (1, 3, 2):
            z_copy(c, i).wait_send()
            x_copy(c, i).wait_send()
        for i in range(3):
            out_copy(i, c).wait()
        return 0

    lax.fori_loop(0, NC, drain2, 0)
    for i in range(1, PEERS):
        rt_copy(i).wait_send()
        g_copy(i).wait_send()
        dg_copy(i).wait_send()
    for i in range(1, SRC):
        dt_copy(i).wait_send()


def call(tok, dy, rt, gain, rwt, wg, wu, wd):
    vmem = pl.BlockSpec(memory_space=pltpu.VMEM)
    hbm = pl.BlockSpec(memory_space=pl.ANY)
    V = pltpu.VMEM
    S = pltpu.SemaphoreType.DMA
    weight = jax.ShapeDtypeStruct((SH, D), BF16)
    return pl.pallas_call(
        kernel,
        out_shape=(
            jax.ShapeDtypeStruct((TOK, D), F32),
            jax.ShapeDtypeStruct((EXPERTS, D), F32),
            jax.ShapeDtypeStruct((8, D), F32),
            weight, weight, weight,
        ),
        in_specs=[vmem] * 5 + [hbm] * 3,
        out_specs=(vmem, vmem, vmem, hbm, hbm, hbm),
        scratch_shapes=[
            V((2 * NC, ROWS, CW), BF16),
            V((2 * NC, ROWS, CW), BF16),
            V((NC, ROWS, CW), BF16),
            V((NC, SH, CW), BF16), V((NC, SH, CW), BF16), V((NC, SH, CW), BF16),
            V((SH, ROWS), F32), V((SH, ROWS), F32),
            V((SH, ROWS), BF16), V((SH, ROWS), BF16), V((SH, ROWS), BF16),
            V((ROWS, SH), BF16), V((ROWS, SH), BF16),
            V((ROWS, ALL), BF16),
            V((8, 8, 128), jnp.int32),
            V((EXPERTS, ALL), F32),
            V((16, ALL), jnp.int32),
            V((8, 8, 256), F32), V((8, 8, 256), F32),
            V((8, 8, 256), F32), V((8, 8, 256), F32),
            V((8, 8, 128), F32), V((SRC, 8, 128), F32),
            V((8, ROWS), F32), V((8, ROWS), F32),
            V((1, ALL), F32), V((EXPERTS, 128), F32),
            V((NC, 8, CW), F32),
            S((3, NC)), S((3, NC)), S((2 * NC,)),
            S((7,)), S((7,)),
            S((2 * NC, 3)), S((2 * NC, 3)), S((2 * NC, 3)), S((2 * NC, 3)),
            S((2 * NC, 7)), S((2 * NC, 7)),
            S((7,)), S((7,)), S((7,)), S((7,)),
            S((15,)), S((15,)),
            S((NC, 7)), S((NC, 7)),
            S((NC, 3)), S((NC, 3)), S((NC, 3)), S((NC, 3)),
            pltpu.SemaphoreType.REGULAR,
        ],
        compiler_params=pltpu.CompilerParams(
            collective_id=0, has_side_effects=True, vmem_limit_bytes=VMEM_LIMIT
        ),
    )(tok, dy, rt, gain, rwt, wg, wu, wd)


VMEM_LIMIT = 65472 * 1024


def local(tokens, out_grad, routes, norm_gain, router_w, w_gate, w_up, w_down):
    rt = jnp.pad(routes[0].T, ((0, 2), (0, 0)), constant_values=-1)
    gain = norm_gain.astype(F32)[None]
    rwt = router_w.T.reshape(EXPERTS, NC, CW).transpose(1, 0, 2)
    gx, grt, gn, gg, gu, gd = call(
        tokens[0], out_grad[0], rt, gain, rwt, w_gate[0], w_up[0], w_down[0]
    )
    both = jnp.concatenate([grt, gn[0:1]], axis=0)
    both = lax.psum(both, ("ts", "dp", "ep"))
    grt = both[0:EXPERTS]
    wide_rw = router_w.astype(F32)
    grad_router = grt.T
    grad_gain = (both[EXPERTS] + jnp.sum(wide_rw * grad_router, axis=1)) / gain[0]
    return (gx[None], gg[None], gu[None], gd[None], grad_router, grad_gain)


def solution(mesh):
    split3 = P(("ts", "ep"), "dp", None)
    return jax.shard_map(
        local,
        mesh=mesh,
        in_specs=(split3, split3, P(("ts", "ep"), None, None), P(), P(), split3, split3, split3),
        out_specs=(split3, split3, split3, split3, P(), P()),
        check_vma=False,
    )
```

time: 833 us -> 454 us (0.55)
  Pallas kernels: 0 us -> 271 us
  blocking collectives: 177 us -> 0 us
  waiting for transfers between devices: 311 us -> 146 us
  matrix products: 107 us -> 0 us
  starting transfers between devices: 79.3 us -> 0.04 us
  local copies, waits for them, and re-layouts: 81.1 us -> 16.9 us
  other arithmetic: 53.2 us -> 5.39 us
    pallas_call x0 -> x1, Pallas kernels: none -> 271 us  [call(): pl.pallas_call(kernel, out_shape=(jax.ShapeDtypeStruct((TOK, D), F32), ja...]
    all_to_all x5 -> x0, waiting for transfers between devices: 217 us -> none  [the longest x1 134 us: local(): lax.all_to_all(row_grads, ('ts', 'ep'), split_axis=0, concat_axis=0, tile...]
    all_gather x2 -> x0, blocking collectives: 111 us -> none  [the longest x1 101 us: local(): lax.all_gather(grad_out, 'dp', axis=0, tiled=True)]
    dot_general x14 -> x0, matrix products: 107 us -> none  [the longest x1 12.5 us: expert_back(): jnp.einsum('secd,efd->secf', recv_u, w_up, preferred_element_type=jnp.flo...]
    all_to_all x5 -> x0, starting transfers between devices: 79.2 us -> none  [the longest x1 25.8 us: local(): lax.all_to_all(send_dy.reshape(groups, exp_dev, bucket_size, model_width)...]
    psum x1, waiting for transfers between devices: 72.8 us -> 146 us  [local(): both = lax.psum(both, ('ts', 'dp', 'ep'))]
    psum x1 -> x0, blocking collectives: 66.5 us -> none  [local(): lax.psum((grad_router, grad_gain), ('ts', 'dp', 'ep'))]
    all_to_all x2 -> x0, other arithmetic: 36.2 us -> none  [the longest x1 35.5 us: local(): lax.all_to_all(row_grads, ('ts', 'ep'), split_axis=0, concat_axis=0, tile...]
  transfers between devices with their start and end apart: 7 -> 1, of which waited for: 4 -> 1; matrix products, arithmetic and copies ran while one was open for 14% -> 0% of each run, Pallas kernels for 0% -> 0%
where the time goes in v1:
time: 454 us; the launch traced here: 453 us
  Pallas kernels  271 us (60%)
  waiting for transfers between devices  146 us (32%)
  local copies, waits for them, and re-layouts  16.9 us (4%)
  between operations  14.1 us (3%)
  other arithmetic  5.39 us (1%)
    pallas_call x1, Pallas kernels, call(): pl.pallas_call(kernel, out_shape=(jax.ShapeDtypeStruct((TOK, D), F32), ja...  271 us
    psum x1, waiting for transfers between devices, local(): both = lax.psum(both, ('ts', 'dp', 'ep'))  146 us
    unnamed x11, local copies, waits for them, and re-layouts  11.4 us
  transfers between devices with their start and end apart: 1, of which 1 were waited for; matrix products, arithmetic and copies ran while one was open for 0% of the time, Pallas kernels for 0%

profile of v1, /device:TPU:1, one launch (start us, length us, event | category | flops | bytes accessed | tf_op | source)
XLA Modules:
  0.0 453.3 jit_solution(14058436236860662412)
XLA Ops:
  7.2 0.0 all-reduce.3.cloned.1.call-start
  7.2 1.7 copy.19
  8.9 1.3 broadcast_in_dim.15.gain
  10.2 0.7 copy.20
  10.9 0.6 pad.4.rt
  11.5 271.0 %shard_map.127 = (f32[64,2560]{1,0:T(8,128)}, f32[64,2560]{1,0:T(8,128)}, f32[8,2560]{1,0:T(8,128)}, bf16[768,2560]{1,0:T(8,128)(2,1)}, bf16[768,2560]{1,0:T(8,128)(2,1)}, /*index=5*/bf16[768,2560]{1,0:T(8,128)(2,1)}) custom-call(bf16[64,2560]{1,0:T(8,128)(2,1)} %bitcast.34, bf16[64,2560]{1,0:T(8,128)(2,1)} %bitcast.35, s32[8,128]{1,0:T(8,128)} %pad.4.rt, ...), custom_call_target="tpu_custom_call" | custom-call | tf_op jit(solution)/shard_map/pallas_call | solution.py:588
  282.5 0.0 copy-start.2
  282.5 1.0 slice.9
  283.5 2.0 pad_maximum_fusion
  285.5 0.0 all-reduce.3.cloned.1.call-update
  285.5 145.9 %all-reduce.3.cloned.1.call-done = f32[65,2560]{1,0:T(8,128)} async-done(((f32[65,2560]{1,0:T(8,128)}), f32[65,2560]{1,0:T(8,128)}) %all-reduce.3.cloned.1.call-update) | async-done | bytes 665616 | tf_op jit(solution)/shard_map/psum | solution.py:643
  431.4 2.1 multiply_reduce_fusion
  433.5 0.9 slice_reduce_fusion
  434.4 1.3 add_divide_fusion
  435.7 0.0 copy-done.2
  435.7 0.8 copy.26
  436.6 0.0 copy-start.1
  436.6 4.4 copy.27
  441.0 0.0 copy-done.1
  441.0 0.0 copy-start
  441.0 2.0 copy.28
  443.0 1.5 copy-done
  444.5 1.9 copy.29
Async XLA Ops:
  7.2 424.3 %all-reduce.3.cloned.1.call-start = ((), (), s32[]{:S(2)}) async-start(), calls=%async_computation | async-start | bytes 1474560 | tf_op jit(solution)/shard_map/psum | solution.py:643
  282.5 153.2 %copy-start.2 = (f32[64,2560]{1,0:T(8,128)S(1)}, f32[64,2560]{1,0:T(8,128)}, u32[]{:S(2)}) copy-start(f32[64,2560]{1,0:T(8,128)} %get-tuple-element.12) | copy-start | bytes 1966084
  436.6 4.4 copy-start.1
  441.0 3.5 copy-start
Sparse Core Ops, SparseCore 0:
  285.6 145.7 all-reduce.2

commit v2 on v1

--- a/solution.py
+++ b/solution.py
@@ -39,10 +39,10 @@
     tok, dy, rt, gain, rwt, wg_in, wu_in, wd_in,
     gx_out, gr_out, gn_out, gg_out, gu_out, gd_out,
     xall, rall, send, wg, wu, wd, acc1, acc2, q, s, h, da, db, pk,
-    rts, zt, slots, gs, gr, ds_, dr, dgt, dgr, gwrow, dgrow, rowg, dzs, gaccum,
+    rts, zt, slots, gs, gr, ds_, dr, dgt, dgr, gwrow, dgrow, rowg, dzs, gaccum, zr, row_s, grt,
     wsem, osem, lsem,
     rt_ss, rt_rs, a_ss, a_rs, b_ss, b_rs, d_ss, d_rs, g_ss, g_rs, dg_ss, dg_rs, dt_ss, dt_rs,
-    r_ss, r_rs, z_ss, z_rs, x_ss, x_rs, free_sem,
+    r_ss, r_rs, z_ss, z_rs, x_ss, x_rs, zb_ss, zb_rs, zs_ss, zs_rs, p1_ss, p1_rs, p2_ss, p2_rs, p3_ss, p3_rs, free_sem,
 ):
     ts, dp, ep = lax.axis_index("ts"), lax.axis_index("dp"), lax.axis_index("ep")
     xh, z = ts // 4, ts % 4
@@ -279,8 +279,8 @@
 
     lax.fori_loop(NC, 2 * NC, drain, 0)
     for i in range(1, 4):
-        pl.semaphore_signal(free_sem, inc=1, device_id=at_xz((z + i) % 4, x), device_id_type=MESH)
-        pl.semaphore_signal(free_sem, inc=1, device_id=at_xz(z, (x + i) % 4), device_id_type=MESH)
+        pl.semaphore_signal(free_sem.at[0], inc=1, device_id=at_xz((z + i) % 4, x), device_id_type=MESH)
+        pl.semaphore_signal(free_sem.at[0], inc=1, device_id=at_xz(z, (x + i) % 4), device_id_type=MESH)
 
     FT = 32
 
@@ -435,10 +435,6 @@
             out_copy(i, c).start()
         return 0
 
-    lax.fori_loop(0, NC, wgrad_body, 0)
-    for c in range(NC):
-        gn_out[:, c * CW : (c + 1) * CW] = gaccum[c]
-
     def dt_copy(i):
         p = (me + i) % SRC
         zz, xx = p // 4, p % 4
@@ -456,71 +452,7 @@
     for i in range(1, SRC):
         dt_copy(i).start()
 
-    pl.semaphore_wait(free_sem, 6)
-
-    def z_copy(c, i):
-        zz = (z + i) % 4
-        return remote(
-            send.at[c, pl.ds(pl.multiple_of(zz * 4 * TOK, 4 * TOK), 4 * TOK)],
-            xall.at[NC + c, pl.ds((i - 1) * 4 * TOK, 4 * TOK)],
-            z_ss.at[c, i - 1],
-            z_rs.at[c, i - 1],
-            at_xz(zz, x),
-        )
-
-    def x_copy(c, i):
-        xx = (x + i) % 4
-        return remote(
-            send.at[c, pl.ds(pl.multiple_of(line + xx * TOK, TOK), TOK)],
-            xall.at[NC + c, pl.ds(12 * TOK + (i - 1) * TOK, TOK)],
-            x_ss.at[c, i - 1],
-            x_rs.at[c, i - 1],
-            at_xz(z, xx),
-        )
-
-    def comb_body(c, _):
-        for i in range(1, PEERS):
-            ret_copy(c, i).wait_recv()
-            ret_copy(c, i).wait_send()
-        own_ret(c).wait()
-
-        def body(i, _):
-            zz = (z + 1 + i) % 4
-            rows = pl.ds(pl.multiple_of(zz * 4 * TOK, 4 * TOK), 4 * TOK)
-            low = dot(da[rows, 0:KA], xall[c, 0:KA, :])
-            send[c, rows, :] = (low + dot(db[rows, 0:KB], xall[c, KA:ROWS, :])).astype(BF16)
-
-            @pl.when(i < 3)
-            def _():
-                z_copy(c, i + 1).start()
-
-            return 0
-
-        lax.fori_loop(0, 4, body, 0)
-        return 0
-
-    def z_sum(c):
-        for i in (1, 3, 2):
-            z_copy(c, i).wait_recv()
-        rows = pl.ds(line, 4 * TOK)
-        tot = send[c, rows, :].astype(F32)
-        for i in range(3):
-            tot = tot + xall[NC + c, i * 4 * TOK : (i + 1) * 4 * TOK, :].astype(F32)
-        send[c, rows, :] = tot.astype(BF16)
-        for i in (1, 3, 2):
-            x_copy(c, i).start()
-
-    def comb_loop(c, _):
-        comb_body(c, 0)
-
-        @pl.when(c > 0)
-        def _():
-            z_sum(c - 1)
-
-        return 0
-
-    lax.fori_loop(0, NC, comb_loop, 0)
-    z_sum(NC - 1)
+    lax.fori_loop(0, 2, wgrad_body, 0)
 
     for i in range(1, SRC):
         dt_copy(i).wait_recv()
@@ -538,16 +470,194 @@
     tot = rowg[0:1, lanes]
     dg = dzs[...]
     mixed = jnp.sum(mask * (sg / tot) * dg, axis=0, keepdims=True)
-    dz = mask * ((dg - mixed) / tot) * sg * (1.0 - sg)
-    pad = jnp.concatenate([dz, jnp.zeros((64, 128), F32)], axis=0)
-    dzs2 = jnp.transpose(pad)
-    acc1[0:128, 0:128] = dzs2
+    dzs[...] = mask * ((dg - mixed) / tot) * sg * (1.0 - sg)
+
+    def zb_copy(i):
+        t = (ts + i) % 8
+        return remote(
+            dzs.at[pl.ds(pl.multiple_of(t * 8, 8), 8)], dgt.at[myb], zb_ss.at[i - 1], zb_rs.at[i - 1], (t, dp, ep)
+        )
+
+    for i in range(1, SRC):
+        dt_copy(i).wait_send()
+    dgt[myb] = dzs[pl.ds(pl.multiple_of(ts * 8, 8), 8), :]
+    for i in range(1, 8):
+        pl.semaphore_signal(free_sem.at[1], inc=1, device_id=((ts + i) % 8, dp, ep), device_id_type=MESH)
+    pl.semaphore_wait(free_sem.at[1], 7)
+    for i in range(1, 8):
+        zb_copy(i).start()
+
+    lax.fori_loop(2, NC, wgrad_body, 0)
+
+    def zs_copy(i):
+        e = (ep + i) % PEERS
+        return remote(gs.at[e], zr.at[ep], zs_ss.at[i - 1], zs_rs.at[i - 1], at_ep(e))
+
+    for i in range(1, 8):
+        zb_copy(i).wait_recv()
+    for i in range(1, PEERS):
+        g_copy(i).wait_send()
+    for d in range(PEERS):
+        got = jnp.zeros((8, MSG), F32)
+        for b in range(8):
+            hi, lo = split(dgt[b])
+            rows = pk[d * MSG : (d + 1) * MSG, b * 128 : (b + 1) * 128]
+            got = got + dot(hi, rows, NT) + dot(lo, rows, NT)
+        gs[d, :, 0:MSG] = got[d : d + 1, :] + jnp.zeros((8, MSG), F32)
+    zr[ep] = gs[ep]
+    for i in range(1, PEERS):
+        zs_copy(i).start()
+
+    def p1_copy(i):
+        e = (ep + i) % PEERS
+        return remote(
+            row_s,
+            acc2.at[pl.ds(pl.multiple_of(ep * 48, 8), 48), pl.ds(0, 128)],
+            p1_ss.at[i - 1],
+            p1_rs.at[i - 1],
+            at_ep(e),
+        )
+
+    def router_row():
+        for i in range(1, PEERS):
+            zs_copy(i).wait_recv()
+        total = jnp.zeros((8, ROWS + 128), F32)
+        zpad = jnp.zeros((8, ROWS + 128 - 256), F32)
+        for e in range(PEERS):
+            piece = jnp.concatenate([zr[e], zpad], axis=1)
+            total = total + (pltpu.roll(piece, e * MSG, 1) if e else piece)
+        hi, lo = split(total[:, 0:ROWS])
+        for c in range(NC):
+            row = (dot(hi, rall[c]) + dot(lo, rall[c]))[0:1, :]
+            part = gaccum[c]
+            for j in range(CW // 128):
+                n = c * (CW // 128) + j
+                row_s[n : n + 1, :] = row[:, j * 128 : (j + 1) * 128]
+                row_s[24 + n : 25 + n, :] = part[0:1, j * 128 : (j + 1) * 128]
+        for i in range(1, PEERS):
+            p1_copy(i).start()
+        acc2[pl.ds(pl.multiple_of(ep * 48, 8), 48), 0:128] = row_s[...]
+
+    myrows = pl.ds(pl.multiple_of(ts * 8, 8), 8)
+
+    def p2_copy(i):
+        return remote(
+            grt.at[myrows], grt.at[myrows], p2_ss.at[i - 1], p2_rs.at[i - 1], ((ts + i) % 8, dp, ep)
+        )
+
+    mygain = pl.ds(pl.multiple_of(me * 24, 8), 24)
+
+    def p3_copy(i):
+        p = (me + i) % SRC
+        block = acc2.at[mygain, pl.ds(128, 128)]
+        return remote(block, block, p3_ss.at[i - 1], p3_rs.at[i - 1], at_xz(p // 4, p % 4))
+
+    def router_rows():
+        for i in range(1, PEERS):
+            p1_copy(i).wait_recv()
+        for n in range(D // 128):
+            rows = [acc2[e * 48 + n : e * 48 + n + 1, 0:128] for e in range(PEERS)]
+            grt[myrows, n * 128 : (n + 1) * 128] = jnp.concatenate(rows, axis=0)
+        tot = acc2[24:48, 0:128]
+        for e in range(1, PEERS):
+            tot = tot + acc2[e * 48 + 24 : (e + 1) * 48, 0:128]
+        acc2[mygain, 128:256] = tot
+        for i in range(1, 8):
+            p2_copy(i).start()
+        for i in range(1, SRC):
+            p3_copy(i).start()
+
+    pl.semaphore_wait(free_sem.at[0], 6)
+
+    def z_copy(c, i):
+        zz = (z + i) % 4
+        return remote(
+            send.at[c, pl.ds(pl.multiple_of(zz * 4 * TOK, 4 * TOK), 4 * TOK)],
+            xall.at[NC + c, pl.ds((i - 1) * 4 * TOK, 4 * TOK)],
+            z_ss.at[c, i - 1],
+            z_rs.at[c, i - 1],
+            at_xz(zz, x),
+        )
+
+    def x_copy(c, i):
+        xx = (x + i) % 4
+        return remote(
+            send.at[c, pl.ds(pl.multiple_of(line + xx * TOK, TOK), TOK)],
+            xall.at[NC + c, pl.ds(12 * TOK + (i - 1) * TOK, TOK)],
+            x_ss.at[c, i - 1],
+            x_rs.at[c, i - 1],
+            at_xz(z, xx),
+        )
+
+    def comb_body(c, _):
+        for i in range(1, PEERS):
+            ret_copy(c, i).wait_recv()
+            ret_copy(c, i).wait_send()
+        own_ret(c).wait()
+
+        def body(i, _):
+            zz = (z + 1 + i) % 4
+            rows = pl.ds(pl.multiple_of(zz * 4 * TOK, 4 * TOK), 4 * TOK)
+            low = dot(da[rows, 0:KA], xall[c, 0:KA, :])
+            send[c, rows, :] = (low + dot(db[rows, 0:KB], xall[c, KA:ROWS, :])).astype(BF16)
+
+            @pl.when(i < 3)
+            def _():
+                z_copy(c, i + 1).start()
+
+            return 0
+
+        lax.fori_loop(0, 4, body, 0)
+        return 0
+
+    def z_sum(c):
+        for i in (1, 3, 2):
+            z_copy(c, i).wait_recv()
+        rows = pl.ds(line, 4 * TOK)
+        tot = send[c, rows, :].astype(F32)
+        for i in range(3):
+            tot = tot + xall[NC + c, i * 4 * TOK : (i + 1) * 4 * TOK, :].astype(F32)
+        send[c, rows, :] = tot.astype(BF16)
+        for i in (1, 3, 2):
+            x_copy(c, i).start()
+
+    def comb_loop(c, _):
+        comb_body(c, 0)
+
+        @pl.when(c > 0)
+        def _():
+            z_sum(c - 1)
+
+        return 0
+
+    comb_loop(0, 0)
+    router_row()
+    lax.fori_loop(1, NC - 1, comb_loop, 0)
+    router_rows()
+    comb_loop(NC - 1, 0)
+    z_sum(NC - 1)
+
+    pad = jnp.concatenate([dzs[...], jnp.zeros((64, 128), F32)], axis=0)
+    acc1[0:128, 0:128] = jnp.transpose(pad)
     dz_own = acc1[pl.ds(pl.multiple_of(dp * TOK, TOK), TOK), 0:EXPERTS]
     hi, lo = split(dz_own)
     wide = tok[...].astype(F32)
     inv = lax.rsqrt(jnp.mean(wide * wide, axis=1, keepdims=True) + 1e-06)
-    u_own = (wide * inv * gain[...]).astype(BF16)
-    gr_out[...] = dot(hi, u_own, TN) + dot(lo, u_own, TN)
+
+    for i in range(1, 8):
+        p2_copy(i).wait_recv()
+    for i in range(1, SRC):
+        p3_copy(i).wait_recv()
+    tot = acc2[0:24, 128:256]
+    for p in range(1, SRC):
+        tot = tot + acc2[p * 24 : (p + 1) * 24, 128:256]
+    for n in range(D // 128):
+        cols = slice(n * 128, (n + 1) * 128)
+        c, o = n * 128 // CW, n * 128 % CW
+        g = grt[:, cols]
+        gr_out[:, cols] = g
+        along = jnp.sum(g * rwt[c, :, o : o + 128].astype(F32), axis=0, keepdims=True)
+        gn_out[:, cols] = (along + tot[n : n + 1, :]) / gain[:, cols]
 
     for c in range(NC):
         cols = slice(c * CW, (c + 1) * CW)
@@ -573,10 +683,13 @@
     lax.fori_loop(0, NC, drain2, 0)
     for i in range(1, PEERS):
         rt_copy(i).wait_send()
-        g_copy(i).wait_send()
         dg_copy(i).wait_send()
+        zb_copy(i).wait_send()
+        zs_copy(i).wait_send()
+        p1_copy(i).wait_send()
+        p2_copy(i).wait_send()
     for i in range(1, SRC):
-        dt_copy(i).wait_send()
+        p3_copy(i).wait_send()
 
 
 def call(tok, dy, rt, gain, rwt, wg, wu, wd):
@@ -590,7 +703,7 @@
         out_shape=(
             jax.ShapeDtypeStruct((TOK, D), F32),
             jax.ShapeDtypeStruct((EXPERTS, D), F32),
-            jax.ShapeDtypeStruct((8, D), F32),
+            jax.ShapeDtypeStruct((1, D), F32),
             weight, weight, weight,
         ),
         in_specs=[vmem] * 5 + [hbm] * 3,
@@ -612,7 +725,7 @@
             V((8, 8, 128), F32), V((SRC, 8, 128), F32),
             V((8, ROWS), F32), V((8, ROWS), F32),
             V((1, ALL), F32), V((EXPERTS, 128), F32),
-            V((NC, 8, CW), F32),
+            V((NC, 8, CW), F32), V((8, 8, 256), F32), V((48, 128), F32), V((EXPERTS, D), F32),
             S((3, NC)), S((3, NC)), S((2 * NC,)),
             S((7,)), S((7,)),
             S((2 * NC, 3)), S((2 * NC, 3)), S((2 * NC, 3)), S((2 * NC, 3)),
@@ -621,7 +734,9 @@
             S((15,)), S((15,)),
             S((NC, 7)), S((NC, 7)),
             S((NC, 3)), S((NC, 3)), S((NC, 3)), S((NC, 3)),
-            pltpu.SemaphoreType.REGULAR,
+            S((7,)), S((7,)), S((7,)), S((7,)), S((7,)), S((7,)),
+            S((7,)), S((7,)), S((15,)), S((15,)),
+            pltpu.SemaphoreType.REGULAR((2,)),
         ],
         compiler_params=pltpu.CompilerParams(
             collective_id=0, has_side_effects=True, vmem_limit_bytes=VMEM_LIMIT
@@ -639,13 +754,7 @@
     gx, grt, gn, gg, gu, gd = call(
         tokens[0], out_grad[0], rt, gain, rwt, w_gate[0], w_up[0], w_down[0]
     )
-    both = jnp.concatenate([grt, gn[0:1]], axis=0)
-    both = lax.psum(both, ("ts", "dp", "ep"))
-    grt = both[0:EXPERTS]
-    wide_rw = router_w.astype(F32)
-    grad_router = grt.T
-    grad_gain = (both[EXPERTS] + jnp.sum(wide_rw * grad_router, axis=1)) / gain[0]
-    return (gx[None], gg[None], gu[None], gd[None], grad_router, grad_gain)
+    return (gx[None], gg[None], gu[None], gd[None], grt.T, gn[0])
 
 
 def solution(mesh):

time: 454 us -> 319 us (0.70)
  waiting for transfers between devices: 146 us -> 0 us
  Pallas kernels: 271 us -> 299 us
  between operations: 14.1 us -> 0.65 us
    psum x1 -> x0, waiting for transfers between devices: 146 us -> none  [local(): both = lax.psum(both, ('ts', 'dp', 'ep'))]
    pallas_call x1, Pallas kernels: 271 us -> 299 us  [call(): pl.pallas_call(kernel, out_shape=(jax.ShapeDtypeStruct((TOK, D), F32), ja...]
    unnamed x11 -> x12, local copies, waits for them, and re-layouts: 11.4 us -> 13.4 us
  transfers between devices with their start and end apart: 1 -> 0, of which waited for: 1 -> 0; matrix products, arithmetic and copies ran while one was open for 0% -> 0% of each run, Pallas kernels for 0% -> 0%
where the time goes in v2:
time: 319 us; the launch traced here: 318 us
  Pallas kernels  299 us (94%)
  local copies, waits for them, and re-layouts  17 us (5%)
    pallas_call x1, Pallas kernels, call(): pl.pallas_call(kernel, out_shape=(jax.ShapeDtypeStruct((TOK, D), F32), ja...  299 us
    unnamed x12, local copies, waits for them, and re-layouts  13.4 us

profile of v2, /device:TPU:1, one launch (start us, length us, event | category | flops | bytes accessed | tf_op | source)
XLA Modules:
  0.0 318.3 jit_solution(17094433876160631433)
XLA Ops:
  0.6 1.7 copy.19
  2.4 1.3 reshape.16.gain
  3.7 0.7 copy.20
  4.3 0.6 pad.4.rt
  4.9 299.3 %shard_map.127 = (f32[64,2560]{1,0:T(8,128)}, f32[64,2560]{1,0:T(8,128)}, f32[1,2560]{1,0:T(1,128)}, bf16[768,2560]{1,0:T(8,128)(2,1)}, bf16[768,2560]{1,0:T(8,128)(2,1)}, /*index=5*/bf16[768,2560]{1,0:T(8,128)(2,1)}) custom-call(bf16[64,2560]{1,0:T(8,128)(2,1)} %bitcast.32, bf16[64,2560]{1,0:T(8,128)(2,1)} %bitcast.33, s32[8,128]{1,0:T(8,128)} %pad.4.rt, ...), custom_call_target="tpu_custom_call" | custom-call | tf_op jit(solution)/shard_map/pallas_call | solution.py:701
  304.3 1.3 reduce
  305.6 2.0 copy.26
  307.6 0.0 copy-start.1
  307.6 4.4 %copy.27 = bf16[1,768,2560]{2,1,0:T(8,128)(2,1)} copy(bf16[1,768,2560]{2,1,0:T(8,128)(2,1)} %bitcast.28) | data formatting | bytes 7864320
  312.0 0.0 copy-done.1
  312.0 0.0 copy-start
  312.0 2.0 copy.28
  314.0 1.5 copy-done
  315.5 0.0 copy-start.2
  315.5 1.9 copy.29
  317.5 0.0 copy-done.2
  317.5 0.8 copy.30
Async XLA Ops:
  307.6 4.4 %copy-start.1 = (bf16[768,2560]{1,0:T(8,128)(2,1)S(1)}, bf16[768,2560]{1,0:T(8,128)(2,1)}, u32[]{:S(2)}) copy-start(bf16[768,2560]{1,0:T(8,128)(2,1)} %get-tuple-element.14) | copy-start | bytes 11796484
  312.0 3.5 %copy-start = (bf16[768,2560]{1,0:T(8,128)(2,1)S(1)}, bf16[768,2560]{1,0:T(8,128)(2,1)}, u32[]{:S(2)}) copy-start(bf16[768,2560]{1,0:T(8,128)(2,1)} %get-tuple-element.15) | copy-start | bytes 11796484
  315.5 1.9 copy-start.2

commit v3 on v2

v3 whole, which is shorter than its diff:
```python
import jax
import jax.numpy as jnp
from jax import lax
from jax.experimental import pallas as pl
from jax.experimental.pallas import tpu as pltpu
from jax.sharding import PartitionSpec as P

MESH = pl.DeviceIdType.MESH
F32 = jnp.float32
BF16 = jnp.bfloat16
D = 2560
NC = 4
CW = D // NC
TOK = 64
MOST = 9
SRC = 16
MSG = SRC * MOST
PEERS = 8
ROWS = PEERS * MSG
ALL = SRC * TOK
SH = 768
EXPERTS = 64
KA = 640
KB = ROWS - KA
NT = (((1,), (1,)), ((), ()))
TN = (((0,), (0,)), ((), ()))


def dot(a, b, dims=(((1,), (0,)), ((), ()))):
    return lax.dot_general(a, b, dims, preferred_element_type=F32)


def split(a):
    hi = a.astype(BF16)
    return hi, (a - hi.astype(F32)).astype(BF16)


def split32(a):
    hi = a.astype(BF16)
    return hi, a - hi.astype(F32)


def kernel(
    tok, dy, rt, gain, rw_in, wg_in, wu_in, wd_in,
    gx_out, gr_out, gn_out, gg_out, gu_out, gd_out,
    xall, rall, send, wg, wu, wd, acc1, acc2, q, s, h, da, db, pk,
    rts, zt, slots, gs, gr, ds_, dr, dgt, dgr, gwrow, dgrow, rowg, dzs, gaccum, zr, row_s, rows8, cols8, rrow,
    wsem, osem, lsem,
    rt_ss, rt_rs, a_ss, a_rs, b_ss, b_rs, f_ss, f_rs, d_ss, d_rs, g_ss, g_rs, dg_ss, dg_rs, dt_ss, dt_rs,
    r_ss, r_rs, z_ss, z_rs, x_ss, x_rs, zb_ss, zb_rs, zs_ss, zs_rs, p1_ss, p1_rs, p2_ss, p2_rs, p3_ss, p3_rs, free_sem,
):
    ts, dp, ep = lax.axis_index("ts"), lax.axis_index("dp"), lax.axis_index("ep")
    xh, z = ts // 4, ts % 4
    x = xh * 2 + dp
    y, core = ep // 2, ep % 2
    g = z * (1 - core) + y * core
    b_at = y * (1 - core) + z * core
    me = g * 4 + x
    tsg = xh * 4 + g
    seat = core * 4 + b_at
    own_d = b_at * 2 + core

    def at_gx(gg, xx):
        zz = gg * (1 - core) + z * core
        yy = y * (1 - core) + gg * core
        return ((xx // 2) * 4 + zz, xx % 2, yy * 2 + core)

    def at_dest(d):
        bb = d // 2
        zz = z * (1 - core) + bb * core
        yy = bb * (1 - core) + y * core
        return (xh * 4 + zz, dp, yy * 2 + d % 2)

    def at_src(e):
        cs, bb = e // 4, e % 4
        zz = z * (1 - cs) + bb * cs
        yy = bb * (1 - cs) + y * cs
        return (xh * 4 + zz, dp, yy * 2 + cs)

    def d_at(e):
        cs = e // 4
        return (y * (1 - cs) + z * cs) * 2 + core

    def rows_of(k):
        return pl.ds(pl.multiple_of(k * MSG, MSG), MSG)

    def others(mine_, act):
        def body(k, _):
            @pl.when(k != mine_)
            def _():
                act(k)

            return 0

        lax.fori_loop(0, PEERS, body, 0)

    def remote(src, dst, ss, rs, dev):
        return pltpu.make_async_remote_copy(
            src_ref=src, dst_ref=dst, send_sem=ss, recv_sem=rs, device_id=dev, device_id_type=MESH
        )

    def wcopy(i, c):
        src, dst = ((wg_in, wg), (wu_in, wu), (wd_in, wd))[i]
        return pltpu.make_async_copy(src.at[:, pl.ds(c * CW, CW)], dst.at[c], wsem.at[i, c])

    for c in range(NC):
        for i in range(3):
            wcopy(i, c).start()

    barrier = pltpu.get_barrier_semaphore()
    def greet(zz, yy, xx, cc):
        pl.semaphore_signal(
            barrier, inc=1, device_id=((xx // 2) * 4 + zz, xx % 2, yy * 2 + cc), device_id_type=MESH
        )

    greet(z, y, x, 1 - core)
    for i in range(1, 4):
        for cc in range(2):
            greet(z, (y + i) % 4, x, cc)
            greet((z + i) % 4, y, x, cc)
    for i in range(4):
        for k in range(1, 4):
            gg = (g + i) % 4
            greet(gg * (1 - core) + z * core, y * (1 - core) + gg * core, (x + k) % 4, core)
    pl.semaphore_wait(barrier, 25)

    myb = g * 2 + xh
    rts[myb] = rt[...]

    def at_tsg(t):
        return at_gx(t % 4, (t // 4) * 2 + dp)

    def rt_copy(i):
        return remote(rt, rts.at[myb], rt_ss.at[i - 1], rt_rs.at[i - 1], at_tsg((tsg + i) % 8))

    for i in range(1, 8):
        rt_copy(i).start()

    def order():
        row = lax.broadcasted_iota(jnp.int32, (EXPERTS, EXPERTS), 0)
        col = lax.broadcasted_iota(jnp.int32, (EXPERTS, EXPERTS), 1)
        turned = (row // 32) * 32 + (row // 2 % 4) * 8 + (row // 8 % 4) * 2 + row % 2
        return jnp.where(col == jnp.where(core == 0, row, turned), 1.0, 0.0).astype(BF16)

    def to_slots():
        cols8[...] = jnp.zeros_like(cols8)
        at = lax.broadcasted_iota(jnp.int32, (16, 128), 1)

        def body(d, _):
            row = rows8[pl.ds(d, 1), :]
            for k in range(MSG // 16):
                hit = pk[pl.ds(pl.multiple_of(d * MSG + k * 16, 16), 16), :].astype(F32)
                one = jnp.sum(hit * row, axis=1, keepdims=True)
                cols8[k * 16 : (k + 1) * 16, :] += jnp.where(at == d, one, 0.0)
            return 0

        lax.fori_loop(0, PEERS, body, 0)
        flat = jnp.transpose(cols8[...])
        for d in range(PEERS):
            gs[d] = flat[d : d + 1, :] + jnp.zeros((8, 256), F32)

    def to_columns(box):
        rows = [box[k][0:1, :] for k in range(PEERS)]
        cols8[...] = jnp.transpose(jnp.concatenate(rows + [jnp.zeros((120, 256), F32)], axis=0))

    def column(k, d):
        part = cols8[k * 16 : (k + 1) * 16, :]
        at = lax.broadcasted_iota(jnp.int32, (16, 128), 1)
        return jnp.sum(jnp.where(at == d, part, 0.0), axis=1, keepdims=True)

    mine = pl.multiple_of(me * TOK, TOK)
    wide = tok[...].astype(F32)
    inv = lax.rsqrt(jnp.mean(wide * wide, axis=1, keepdims=True) + 1e-06)
    u_own = (wide * inv * gain[...]).astype(BF16)
    for c in range(NC):
        xall[c, pl.ds(mine, TOK), :] = u_own[:, c * CW : (c + 1) * CW]
        xall[NC + c, pl.ds(mine, TOK), :] = dy[:, c * CW : (c + 1) * CW]

    line = pl.multiple_of(g * 4 * TOK, 4 * TOK)

    def a_copy(st, i, along_x):
        block = xall.at[st, pl.ds(mine, TOK)]
        dev = at_gx(g, (x + i) % 4) if along_x else at_gx((g + i) % 4, x)
        return remote(block, block, a_ss.at[st, i - 1], a_rs.at[st, i - 1], dev)

    def side(i, along_x):
        return at_gx(g, (x + i) % 4) if along_x else at_gx((g + i) % 4, x)

    def b_line(st, i):
        block = xall.at[st, pl.ds(line, 4 * TOK)]
        return remote(block, block, b_ss.at[st, i // 2], b_rs.at[st, i // 2], side(i, False))

    def b_piece(st, i, k):
        block = xall.at[st, pl.ds(pl.multiple_of((k * 4 + x) * TOK, TOK), TOK)]
        return remote(block, block, b_ss.at[st, i // 2], b_rs.at[st, i // 2], side(i, True))

    def f_line(st, i):
        at = (g - i + 4) % 4 * 4 * TOK + (i // 2) * 2 * TOK
        block = xall.at[st, pl.ds(pl.multiple_of(at, TOK), 2 * TOK)]
        return remote(block, block, f_ss.at[st, i // 2], f_rs.at[st, i // 2], side(i, False))

    def f_piece(st, i, k):
        at = ((k + (i // 2) * 2) * 4 + (x - i + 4) % 4) * TOK
        block = xall.at[st, pl.ds(pl.multiple_of(at, TOK), TOK)]
        return remote(block, block, f_ss.at[st, i // 2], f_rs.at[st, i // 2], side(i, True))

    def first(st):
        for i in (1, 3, 2):
            a_copy(st, i, st == 0).start()

    def forward(st):
        for i in (1, 3, 2):
            a_copy(st, i, True).wait_recv()

        @pl.when(st == 0)
        def _():
            for i in (1, 3):
                b_line(st, i).start()

        @pl.when(st != 0)
        def _():
            for i in (1, 3):
                for k in range(4):
                    b_piece(st, i, k).start()

    def onward(st):
        for i in (1, 3):
            b_line(st, i).wait_recv()

            @pl.when(st == 0)
            def _():
                f_line(st, i).start()

            @pl.when(st != 0)
            def _():
                for k in range(2):
                    f_piece(st, i, k).start()

    for st in range(4):
        first(st)
    forward(0)
    forward(1)
    forward(2)
    for st in range(4, 2 * NC):
        first(st)
    for i in range(1, 8):
        rt_copy(i).wait_recv()
    lane = lax.broadcasted_iota(jnp.int32, (128, 128), 1)
    sub = lax.broadcasted_iota(jnp.int32, (128, 128), 0)
    before = jnp.where((sub < lane) & ((sub // TOK) == (lane // TOK)), 1.0, 0.0).astype(BF16)
    for b in range(8):
        r = rts[b]
        ids = lax.broadcasted_iota(jnp.int32, (16, 128), 0)
        own = jnp.zeros((16, 128), F32)
        for k in range(6):
            own = own + jnp.where((r[k : k + 1, :] == tsg * PEERS + ids) & (ids < PEERS), 1.0, 0.0)
        rank = dot(own.astype(BF16), before)
        half = lax.broadcasted_iota(jnp.int32, (16, 128), 1) // TOK
        slot = jnp.where(own > 0.5, (2 * b + half) * MOST + rank.astype(jnp.int32), -1)
        slots[:, b * 128 : (b + 1) * 128] = slot

    def slot_body(d, _):
        row = slots[pl.ds(d, 1), :]
        hit = lax.broadcasted_iota(jnp.int32, (MSG, ALL), 0) == row
        pk[pl.ds(pl.multiple_of(d * MSG, MSG), MSG), :] = jnp.where(hit, 1.0, 0.0).astype(BF16)
        return 0

    lax.fori_loop(0, PEERS, slot_body, 0)
    onward(0)
    def d_copy(st, d):
        return remote(
            send.at[st % NC, rows_of(d)], rall.at[st, rows_of(seat)], d_ss.at[st, d], d_rs.at[st, seat], at_dest(d)
        )

    def d_arrival(st, e):
        return remote(send.at[st % NC, rows_of(e)], rall.at[st, rows_of(e)], d_ss.at[st, e], d_rs.at[st, e], at_src(e))

    def own_copy(st):
        return pltpu.make_async_copy(send.at[st % NC, rows_of(own_d)], rall.at[st, rows_of(seat)], lsem.at[st])

    def pack(st):
        for i in (1, 3):
            f_line(st, i).wait_recv()

        def body(i, _):
            bb = (b_at + 1 + i) % 4
            rows = pl.ds(pl.multiple_of(bb * 2 * MSG, 2 * MSG), 2 * MSG)
            send[st % NC, rows, :] = dot(pk[rows, :], xall[st, pl.ds(0, ALL), :]).astype(BF16)
            for cc in range(2):
                d = bb * 2 + cc

                @pl.when(d != own_d)
                def _():
                    d_copy(st, d).start()

            return 0

        lax.fori_loop(0, 4, body, 0)
        own_copy(st).start()

        @pl.when(st + 1 < 2 * NC)
        def _():
            onward(st + 1)

    def gathered(st):
        for i in (1, 3, 2):
            a_copy(st, i, True).wait_send()
        for i in (1, 3):
            b_line(st, i).wait_send()
            f_line(st, i).wait_send()

    def u_body(c, _):
        forward(c + 3)
        pack(c)
        rw = dot(order(), rw_in[:, pl.ds(pl.multiple_of(c * CW, CW), CW)]).astype(BF16)
        part = dot(rw, xall[c, pl.ds(0, ALL), :], NT)

        @pl.when(c == 0)
        def _():
            zt[...] = part

        @pl.when(c > 0)
        def _():
            zt[...] += part

        return 0

    lax.fori_loop(0, NC, u_body, 0)

    for b in range(8):
        lanes = slice(b * 128, (b + 1) * 128)
        r = rts[b]
        ids = lax.broadcasted_iota(jnp.int32, (EXPERTS, 128), 0)
        mask = jnp.zeros((EXPERTS, 128), F32)
        for k in range(6):
            mask = mask + jnp.where(r[k : k + 1, :] == ids, 1.0, 0.0)
        sg = jax.nn.sigmoid(zt[:, lanes])
        zt[:, lanes] = sg
        rowg[:, lanes] = jnp.sum(mask * sg, axis=0, keepdims=True)
    gt = (zt[pl.ds(pl.multiple_of(tsg * PEERS, PEERS), PEERS), :] / rowg[...]).astype(BF16)

    def g_copy(d):
        return remote(gs.at[d], gr.at[seat], g_ss.at[d], g_rs.at[seat], at_dest(d))

    def g_arrival(e):
        return remote(gs.at[e], gr.at[e], g_ss.at[e], g_rs.at[e], at_src(e))

    rows8[...] = gt.astype(F32)
    to_slots()
    gr[seat] = gs[own_d]
    others(own_d, lambda d: g_copy(d).start())

    def wait_d(st):
        others(seat, lambda e: d_arrival(st, e).wait_recv())
        own_copy(st).wait()

    NTILE = ROWS // 3

    def ab_body(c, _):
        others(own_d, lambda d: d_copy(c, d).wait_send())

        @pl.when(c + 3 < NC)
        def _():
            forward(NC + c + 3)

        wait_d(c)
        gathered(c)
        pack(NC + c)
        for i in range(2):
            wcopy_dyn(i, c).wait()

        def tile(t, _):
            cols = pl.ds(pl.multiple_of(t * NTILE, NTILE), NTILE)
            rows = rall[c, cols, :]
            pa = dot(wg[c], rows, NT)
            pb = dot(wu[c], rows, NT)

            @pl.when(c == 0)
            def _():
                acc1[:, cols] = pa
                acc2[:, cols] = pb

            @pl.when(c > 0)
            def _():
                acc1[:, cols] += pa
                acc2[:, cols] += pb

            return 0

        lax.fori_loop(0, 3, tile, 0)
        return 0

    def wcopy_dyn(i, c):
        src, dst = ((wg_in, wg), (wu_in, wu), (wd_in, wd))[i]
        return pltpu.make_async_copy(
            src.at[:, pl.ds(pl.multiple_of(c * CW, CW), CW)], dst.at[c], wsem.at[i, c]
        )

    lax.fori_loop(0, NC, ab_body, 0)

    def drain(st, _):
        gathered(st)
        return 0

    lax.fori_loop(NC, 2 * NC, drain, 0)
    for i in range(1, 4):
        for dev in (at_gx((g + i) % 4, x), at_gx(g, (x + i) % 4)):
            pl.semaphore_signal(free_sem.at[0], inc=1, device_id=dev, device_id_type=MESH)

    FT = 32

    def act_body(t, _):
        f = pl.ds(pl.multiple_of(t * FT, FT), FT)
        a, b = acc1[f, :], acc2[f, :]
        sg = jax.nn.sigmoid(a)
        act = a * sg
        h[f, :] = (act * b).astype(BF16)
        s[f, :] = act.astype(BF16)
        q[f, :] = (b * sg * (1.0 + a * (1.0 - sg))).astype(BF16)
        return 0

    lax.fori_loop(0, SH // FT, act_body, 0)

    others(seat, lambda e: g_arrival(e).wait_recv())
    total = jnp.zeros((8, ROWS + 128), F32)
    zpad = jnp.zeros((8, ROWS + 128 - 256), F32)
    for e in range(PEERS):
        piece = jnp.concatenate([gr[e], zpad], axis=1)
        total = total + (pltpu.roll(piece, e * MSG, 1) if e else piece)
    gwrow[...] = total[:, 0:ROWS]

    def p_body(c, _):
        wait_d(NC + c)
        wcopy_dyn(2, c).wait()

        def tile(t, _):
            cols = pl.ds(pl.multiple_of(t * NTILE, NTILE), NTILE)
            pp = dot(wd[c], rall[NC + c, cols, :], NT)

            @pl.when(c == 0)
            def _():
                acc1[:, cols] = pp

            @pl.when(c > 0)
            def _():
                acc1[:, cols] += pp

            return 0

        lax.fori_loop(0, 3, tile, 0)
        return 0

    lax.fori_loop(0, NC, p_body, 0)

    dgrow[...] = jnp.zeros_like(dgrow)
    GT = 128

    def grad_body(t, _):
        f = pl.ds(pl.multiple_of(t * GT, GT), GT)
        part = jnp.zeros((8, ROWS), F32)
        gw = gwrow[0:1, :]
        for k in range(GT // 16):
            fk = pl.ds(pl.multiple_of(t * GT + k * 16, 16), 16)
            p = acc1[fk, :]
            hh = h[fk, :].astype(F32)
            prod = hh * p
            part = part + prod[0:8] + prod[8:16]
            dh = p * gw
            q[fk, :] = (dh * q[fk, :].astype(F32)).astype(BF16)
            s[fk, :] = (dh * s[fk, :].astype(F32)).astype(BF16)
            h[fk, :] = (hh * gw).astype(BF16)
        dgrow[...] += part
        da[:, f] = jnp.transpose(q[f, :])
        db[:, f] = jnp.transpose(s[f, :])
        return 0

    lax.fori_loop(0, SH // GT, grad_body, 0)

    def dg_copy(e):
        return remote(ds_.at[e], dr.at[d_at(e)], dg_ss.at[e], dg_rs.at[d_at(e)], at_src(e))

    def dg_arrival(d):
        return remote(ds_.at[d], dr.at[d], dg_ss.at[d], dg_rs.at[d], at_dest(d))

    dg = jnp.sum(dgrow[...], axis=0, keepdims=True) + jnp.zeros((8, ROWS), F32)
    dg = jnp.concatenate([dg, jnp.zeros((8, 128), F32)], axis=1)
    keep = lax.broadcasted_iota(jnp.int32, (8, 256), 1) < MSG
    for e in range(PEERS):
        moved = pltpu.roll(dg, ROWS + 128 - e * MSG, 1) if e else dg
        ds_[e] = jnp.where(keep, moved[:, 0:256], 0.0)
    dr[own_d] = ds_[seat]
    others(seat, lambda e: dg_copy(e).start())

    def ret_copy(c, e):
        return remote(
            send.at[c, rows_of(e)], xall.at[c, rows_of(d_at(e))], r_ss.at[c, e], r_rs.at[c, d_at(e)], at_src(e)
        )

    def ret_arrival(c, d):
        return remote(send.at[c, rows_of(d)], xall.at[c, rows_of(d)], r_ss.at[c, d], r_rs.at[c, d], at_dest(d))

    def own_ret(c):
        return pltpu.make_async_copy(send.at[c, rows_of(seat)], xall.at[c, rows_of(own_d)], lsem.at[c])

    def ret_body(c, _):
        others(own_d, lambda d: d_copy(NC + c, d).wait_send())

        def body(i, _):
            m = (seat // 2 + 1 + i) % 4
            rows = pl.ds(pl.multiple_of(m * 2 * MSG, 2 * MSG), 2 * MSG)
            send[c, rows, :] = (dot(da[rows, :], wg[c]) + dot(db[rows, :], wu[c])).astype(BF16)
            for cc in range(2):
                e = m * 2 + cc

                @pl.when(e != seat)
                def _():
                    ret_copy(c, e).start()

            return 0

        lax.fori_loop(0, 4, body, 0)
        own_ret(c).start()
        return 0

    def out_copy(i, c):
        src, dst = ((wg, gg_out), (wu, gu_out), (wd, gd_out))[i]
        return pltpu.make_async_copy(
            src.at[c], dst.at[:, pl.ds(pl.multiple_of(c * CW, CW), CW)], osem.at[i, c]
        )

    MT = 256

    def wgrad_body(c, _):
        gaccum[c] = jnp.zeros((8, CW), F32)

        def tile(t, _):
            f = pl.ds(pl.multiple_of(t * MT, MT), MT)
            ga = dot(q[f, :], rall[c])
            part = jnp.sum(ga * wg[c, f, :].astype(F32), axis=0, keepdims=True)
            wg[c, f, :] = ga.astype(BF16)
            gb = dot(s[f, :], rall[c])
            part = part + jnp.sum(gb * wu[c, f, :].astype(F32), axis=0, keepdims=True)
            wu[c, f, :] = gb.astype(BF16)
            gaccum[c] += part + jnp.zeros((8, CW), F32)
            wd[c, f, :] = dot(h[f, :], rall[NC + c]).astype(BF16)
            return 0

        lax.fori_loop(0, SH // MT, tile, 0)
        for i in range(3):
            out_copy(i, c).start()
        return 0

    ret_body(0, 0)

    def dt_copy(i):
        p = (me + i) % SRC
        gg, xx = p // 4, p % 4
        return remote(dgt.at[gg * 2 + xx // 2], dgr.at[me], dt_ss.at[i - 1], dt_rs.at[i - 1], at_gx(gg, xx))

    others(own_d, lambda d: dg_arrival(d).wait_recv())
    to_columns(dr)

    def dgt_body(d, _):
        got = jnp.zeros((1, ALL), F32)
        for k in range(MSG // 16):
            hit = pk[pl.ds(pl.multiple_of(d * MSG + k * 16, 16), 16), :].astype(F32)
            got = got + jnp.sum(hit * column(k, d), axis=0, keepdims=True)
        for b in range(8):
            dgt[b, pl.ds(d, 1), :] = got[:, b * 128 : (b + 1) * 128]
        return 0

    lax.fori_loop(0, PEERS, dgt_body, 0)
    dgr[me] = dgt[myb]
    for i in range(1, SRC):
        dt_copy(i).start()

    ret_body(1, 0)

    for i in range(1, SRC):
        dt_copy(i).wait_recv()
    for t in range(8):
        zz, hh = t % 4, t // 4
        j = zz * 4 + hh * 2
        dzs[t * 8 : (t + 1) * 8, :] = dgr[j] + dgr[j + 1]
    lanes = pl.ds(pl.multiple_of(myb * 128, 128), 128)
    r = rt[...]
    ids = lax.broadcasted_iota(jnp.int32, (EXPERTS, 128), 0)
    mask = jnp.zeros((EXPERTS, 128), F32)
    for k in range(6):
        mask = mask + jnp.where(r[k : k + 1, :] == ids, 1.0, 0.0)
    sg = zt[:, lanes]
    tot = rowg[0:1, lanes]
    dg = dzs[...]
    mixed = jnp.sum(mask * (sg / tot) * dg, axis=0, keepdims=True)
    dzs[...] = mask * ((dg - mixed) / tot) * sg * (1.0 - sg)

    def zb_copy(i):
        t = (tsg + i) % 8
        return remote(
            dzs.at[pl.ds(pl.multiple_of(t * 8, 8), 8)], dgt.at[myb], zb_ss.at[i - 1], zb_rs.at[i - 1], at_tsg(t)
        )

    for i in range(1, SRC):
        dt_copy(i).wait_send()
    dgt[myb] = dzs[pl.ds(pl.multiple_of(tsg * 8, 8), 8), :]
    for i in range(1, 8):
        pl.semaphore_signal(free_sem.at[1], inc=1, device_id=at_tsg((tsg + i) % 8), device_id_type=MESH)
    pl.semaphore_wait(free_sem.at[1], 7)
    for i in range(1, 8):
        zb_copy(i).start()

    lax.fori_loop(2, NC - 1, ret_body, 0)

    def zs_copy(d):
        return remote(gs.at[d], zr.at[seat], zs_ss.at[d], zs_rs.at[seat], at_dest(d))

    def zs_arrival(e):
        return remote(gs.at[e], zr.at[e], zs_ss.at[e], zs_rs.at[e], at_src(e))

    for i in range(1, 8):
        zb_copy(i).wait_recv()
    others(own_d, lambda d: g_copy(d).wait_send())
    for b in range(8):
        rows8[:, b * 128 : (b + 1) * 128] = dgt[b]
    to_slots()
    zr[seat] = gs[own_d]
    others(own_d, lambda d: zs_copy(d).start())
    ret_body(NC - 1, 0)

    for b in range(8):
        lanes = slice(b * 128, (b + 1) * 128)
        da[lanes, 0:KA] = jnp.transpose(pk[0:KA, lanes])
        db[lanes, 0:KB] = jnp.transpose(pk[KA:ROWS, lanes])

    def p1_rows(d):
        return acc2.at[pl.ds(pl.multiple_of(d * 48, 8), 48), pl.ds(0, 128)]

    def p1_copy(e):
        return remote(row_s, p1_rows(d_at(e)), p1_ss.at[e], p1_rs.at[d_at(e)], at_src(e))

    def p1_arrival(d):
        return remote(row_s, p1_rows(d), p1_ss.at[d], p1_rs.at[d], at_dest(d))

    def router_row():
        others(seat, lambda e: zs_arrival(e).wait_recv())
        to_columns(zr)
        rrow[...] = jnp.zeros_like(rrow)

        def body(e, _):
            for k in range(MSG // 16):
                one = column(k, e)
                for c in range(NC):
                    rows = rall[c, pl.ds(pl.multiple_of(e * MSG + k * 16, 16), 16), :].astype(F32) * one
                    rrow[c] += rows[0:8] + rows[8:16]
            return 0

        lax.fori_loop(0, PEERS, body, 0)
        for c in range(NC):
            row = jnp.sum(rrow[c], axis=0, keepdims=True)
            part = gaccum[c]
            for j in range(CW // 128):
                n = c * (CW // 128) + j
                row_s[n : n + 1, :] = row[:, j * 128 : (j + 1) * 128]
                row_s[24 + n : 25 + n, :] = part[0:1, j * 128 : (j + 1) * 128]
        others(seat, lambda e: p1_copy(e).start())
        acc2[pl.ds(pl.multiple_of(own_d * 48, 8), 48), 0:128] = row_s[...]

    def grt(c, k, n):
        return acc2.at[pl.ds(pl.multiple_of(c * EXPERTS + k * 8, 8), 8 * n), pl.ds(256, CW)]

    def p2_copy(i, c):
        block = grt(c, tsg, 1)
        return remote(block, block, p2_ss.at[i - 1], p2_rs.at[i - 1], at_tsg((tsg + i) % 8))

    def p2_all(i):
        block = grt(0, 0, NC)
        return remote(block, block, p2_ss.at[i - 1], p2_rs.at[i - 1], at_tsg((tsg + i) % 8))

    mygain = pl.ds(pl.multiple_of(me * 24, 8), 24)

    def p3_copy(i):
        p = (me + i) % SRC
        block = acc2.at[mygain, pl.ds(128, 128)]
        return remote(block, block, p3_ss.at[i - 1], p3_rs.at[i - 1], at_gx(p // 4, p % 4))

    def router_rows():
        others(own_d, lambda d: p1_arrival(d).wait_recv())
        for n in range(D // 128):
            rows = [acc2[e * 48 + n : e * 48 + n + 1, 0:128] for e in range(PEERS)]
            c, o = n * 128 // CW, 256 + n * 128 % CW
            at = pl.ds(pl.multiple_of(c * EXPERTS + tsg * 8, 8), 8)
            acc2[at, o : o + 128] = jnp.concatenate(rows, axis=0)
        tot = acc2[24:48, 0:128]
        for e in range(1, PEERS):
            tot = tot + acc2[e * 48 + 24 : (e + 1) * 48, 0:128]
        acc2[mygain, 128:256] = tot
        for i in range(1, 8):
            for c in range(NC):
                p2_copy(i, c).start()
        for i in range(1, SRC):
            p3_copy(i).start()

    pl.semaphore_wait(free_sem.at[0], 6)


    def z_line(c, i):
        gg = (g + i) % 4
        return remote(
            send.at[c, pl.ds(pl.multiple_of(gg * 4 * TOK, 4 * TOK), 4 * TOK)],
            xall.at[NC + c, pl.ds((i - 1) * 4 * TOK, 4 * TOK)],
            z_ss.at[c, i - 1],
            z_rs.at[c, i - 1],
            at_gx(gg, x),
        )

    def z_piece(c, i, k):
        xx = (x + i) % 4
        return remote(
            send.at[c, pl.ds(pl.multiple_of((k * 4 + xx) * TOK, TOK), TOK)],
            xall.at[NC + c, pl.ds(pl.multiple_of((i - 1) * 4 * TOK + k * TOK, TOK), TOK)],
            z_ss.at[c, i - 1],
            z_rs.at[c, i - 1],
            at_gx(g, xx),
        )

    def x_copy(c, i, along_x):
        xx, gg = ((x + i) % 4, g) if along_x else (x, (g + i) % 4)
        return remote(
            send.at[c, pl.ds(pl.multiple_of((gg * 4 + xx) * TOK, TOK), TOK)],
            xall.at[NC + c, pl.ds(12 * TOK + (i - 1) * TOK, TOK)],
            x_ss.at[c, i - 1],
            x_rs.at[c, i - 1],
            at_gx(gg, xx),
        )

    def comb_body(c):
        others(own_d, lambda d: ret_arrival(c, d).wait_recv())
        others(seat, lambda e: ret_copy(c, e).wait_send())
        own_ret(c).wait()

        def body(i, _):
            gg = (g + 1 + i) % 4
            rows = pl.ds(pl.multiple_of(gg * 4 * TOK, 4 * TOK), 4 * TOK)
            low = dot(da[rows, 0:KA], xall[c, 0:KA, :])
            send[c, rows, :] = (low + dot(db[rows, 0:KB], xall[c, KA:ROWS, :])).astype(BF16)

            @pl.when((i < 3) & (c >= 2))
            def _():
                z_line(c, i + 1).start()

            @pl.when(c < 2)
            def _():
                for k in (1, 3, 2):
                    z_piece(c, k, gg).start()

            return 0

        lax.fori_loop(0, 4, body, 0)

    def z_sum(c):
        for i in (1, 3, 2):
            z_line(c, i).wait_recv()

        def body(k, _):
            row = jnp.where(c >= 2, g * 4 + k, k * 4 + x) * TOK
            rows = pl.ds(pl.multiple_of(row, TOK), TOK)
            tot = send[c, rows, :].astype(F32)
            for i in range(3):
                part = pl.ds(pl.multiple_of((i * 4 + k) * TOK, TOK), TOK)
                tot = tot + xall[NC + c, part, :].astype(F32)
            send[c, rows, :] = tot.astype(BF16)
            return 0

        lax.fori_loop(0, 4, body, 0)

        @pl.when(c >= 2)
        def _():
            for i in (1, 3, 2):
                x_copy(c, i, True).start()

        @pl.when(c < 2)
        def _():
            for i in (1, 3, 2):
                x_copy(c, i, False).start()

    comb_body(0)
    wgrad_body(0, 0)
    comb_body(1)
    z_sum(0)
    lax.fori_loop(1, 3, wgrad_body, 0)
    comb_body(2)
    z_sum(1)
    wgrad_body(3, 0)
    router_row()
    comb_body(3)
    z_sum(2)
    router_rows()
    z_sum(3)

    pad = jnp.concatenate([dzs[...], jnp.zeros((64, 128), F32)], axis=0)
    acc1[0:128, 0:128] = jnp.transpose(pad)
    dz_own = acc1[pl.ds(pl.multiple_of(dp * TOK, TOK), TOK), 0:EXPERTS]
    hi, lo = split(dz_own)
    both = dot(jnp.concatenate([hi, lo], axis=0), order()).astype(BF16)
    for c in range(NC):
        cols = slice(c * CW, (c + 1) * CW)
        two = dot(both, rw_in[:, cols])
        gx_out[:, cols] = two[0:TOK] + two[TOK : 2 * TOK]
    wide = tok[...].astype(F32)
    inv = lax.rsqrt(jnp.mean(wide * wide, axis=1, keepdims=True) + 1e-06)

    for i in range(1, 8):
        p2_all(i).wait_recv()
    for i in range(1, SRC):
        p3_copy(i).wait_recv()
    tot = acc2[0:24, 128:256]
    for p in range(1, SRC):
        tot = tot + acc2[p * 24 : (p + 1) * 24, 128:256]
    thrice = jnp.concatenate([order()] * 3, axis=1)
    for c in range(NC):
        rest = acc2[c * EXPERTS : (c + 1) * EXPERTS, 256 : 256 + CW]
        parts = []
        for _ in range(3):
            hi, rest = split32(rest)
            parts.append(hi)
        gr_out[:, c * CW : (c + 1) * CW] = dot(thrice, jnp.concatenate(parts, axis=0))
    for n in range(D // 128):
        cols = slice(n * 128, (n + 1) * 128)
        along = jnp.sum(gr_out[:, cols] * rw_in[:, cols].astype(F32), axis=0, keepdims=True)
        gn_out[:, cols] = (along + tot[n : n + 1, :]) / gain[:, cols]

    for c in range(NC):
        cols = slice(c * CW, (c + 1) * CW)
        du = gx_out[:, cols]
        for i in (1, 3, 2):
            x_copy(c, i, True).wait_recv()
        du = du + send[c, pl.ds(mine, TOK), :].astype(F32)
        for i in range(3):
            du = du + xall[NC + c, (12 + i) * TOK : (13 + i) * TOK, :].astype(F32)
        gx_out[:, cols] = du * gain[:, cols]
    v = wide * inv
    scaled = gx_out[...]
    gx_out[...] = inv * scaled - v * inv * jnp.mean(v * scaled, axis=1, keepdims=True)

    def drain2(c, _):
        for i in (1, 3, 2):
            z_line(c, i).wait_send()
            x_copy(c, i, True).wait_send()
        for i in range(3):
            out_copy(i, c).wait()
        return 0

    lax.fori_loop(0, NC, drain2, 0)
    for i in range(1, 8):
        rt_copy(i).wait_send()
        zb_copy(i).wait_send()
        p2_all(i).wait_send()
    others(own_d, lambda d: zs_copy(d).wait_send())
    others(seat, lambda e: dg_copy(e).wait_send())
    others(seat, lambda e: p1_copy(e).wait_send())
    for i in range(1, SRC):
        p3_copy(i).wait_send()


def call(tok, dy, rt, gain, rwt, wg, wu, wd):
    vmem = pl.BlockSpec(memory_space=pltpu.VMEM)
    hbm = pl.BlockSpec(memory_space=pl.ANY)
    V = pltpu.VMEM
    S = pltpu.SemaphoreType.DMA
    weight = jax.ShapeDtypeStruct((SH, D), BF16)
    return pl.pallas_call(
        kernel,
        out_shape=(
            jax.ShapeDtypeStruct((TOK, D), F32),
            jax.ShapeDtypeStruct((EXPERTS, D), F32),
            jax.ShapeDtypeStruct((1, D), F32),
            weight, weight, weight,
        ),
        in_specs=[vmem] * 5 + [hbm] * 3,
        out_specs=(vmem, vmem, vmem, hbm, hbm, hbm),
        scratch_shapes=[
            V((2 * NC, ROWS, CW), BF16),
            V((2 * NC, ROWS, CW), BF16),
            V((NC, ROWS, CW), BF16),
            V((NC, SH, CW), BF16), V((NC, SH, CW), BF16), V((NC, SH, CW), BF16),
            V((SH, ROWS), F32), V((SH, ROWS), F32),
            V((SH, ROWS), BF16), V((SH, ROWS), BF16), V((SH, ROWS), BF16),
            V((ROWS, SH), BF16), V((ROWS, SH), BF16),
            V((ROWS, ALL), BF16),
            V((8, 8, 128), jnp.int32),
            V((EXPERTS, ALL), F32),
            V((16, ALL), jnp.int32),
            V((8, 8, 256), F32), V((8, 8, 256), F32),
            V((8, 8, 256), F32), V((8, 8, 256), F32),
            V((8, 8, 128), F32), V((SRC, 8, 128), F32),
            V((8, ROWS), F32), V((8, ROWS), F32),
            V((1, ALL), F32), V((EXPERTS, 128), F32),
            V((NC, 8, CW), F32), V((8, 8, 256), F32), V((48, 128), F32), V((8, ALL), F32), V((256, 128), F32), V((NC, 8, CW), F32),
            S((3, NC)), S((3, NC)), S((2 * NC,)),
            S((7,)), S((7,)),
            S((2 * NC, 3)), S((2 * NC, 3)), S((2 * NC, 2)), S((2 * NC, 2)), S((2 * NC, 2)), S((2 * NC, 2)),
            S((2 * NC, 8)), S((2 * NC, 8)),
            S((8,)), S((8,)), S((8,)), S((8,)),
            S((15,)), S((15,)),
            S((NC, 8)), S((NC, 8)),
            S((NC, 3)), S((NC, 3)), S((NC, 3)), S((NC, 3)),
            S((7,)), S((7,)), S((8,)), S((8,)), S((8,)), S((8,)),
            S((7,)), S((7,)), S((15,)), S((15,)),
            pltpu.SemaphoreType.REGULAR((2,)),
        ],
        compiler_params=pltpu.CompilerParams(
            collective_id=0, has_side_effects=True, vmem_limit_bytes=VMEM_LIMIT
        ),
    )(tok, dy, rt, gain, rwt, wg, wu, wd)


VMEM_LIMIT = 65472 * 1024


def local(tokens, out_grad, routes, norm_gain, router_w, w_gate, w_up, w_down):
    core = lax.axis_index("ep") % 2
    ids = routes[0].T
    turned = (ids // 32) * 32 + (ids // 2 % 4) * 8 + (ids // 8 % 4) * 2 + ids % 2
    rt = jnp.pad(jnp.where(core == 0, ids, turned), ((0, 2), (0, 0)), constant_values=-1)
    gain = norm_gain.astype(F32)[None]

    gx, grt, gn, gg, gu, gd = call(
        tokens[0], out_grad[0], rt, gain, router_w.T, w_gate[0], w_up[0], w_down[0]
    )
    return (gx[None], gg[None], gu[None], gd[None], grt.T, gn[0])


def solution(mesh):
    split3 = P(("ts", "ep"), "dp", None)
    return jax.shard_map(
        local,
        mesh=mesh,
        in_specs=(split3, split3, P(("ts", "ep"), None, None), P(), P(), split3, split3, split3),
        out_specs=(split3, split3, split3, split3, P(), P()),
        check_vma=False,
    )
```

time: 319 us -> 235 us (0.74)
  Pallas kernels: 299 us -> 217 us
    pallas_call x1, Pallas kernels: 299 us -> 217 us  [call(): pl.pallas_call(kernel, out_shape=(jax.ShapeDtypeStruct((TOK, D), F32), ja...]
    unnamed x12 -> x11, local copies, waits for them, and re-layouts: 13.4 us -> 12.7 us
where the time goes in v3:
time: 235 us; the launch traced here: 234 us
  Pallas kernels  217 us (92%)
  local copies, waits for them, and re-layouts  14.6 us (6%)
    pallas_call x1, Pallas kernels, call(): pl.pallas_call(kernel, out_shape=(jax.ShapeDtypeStruct((TOK, D), F32), ja...  217 us
    unnamed x11, local copies, waits for them, and re-layouts  12.7 us

profile of v3, /device:TPU:1, one launch (start us, length us, event | category | flops | bytes accessed | tf_op | source)
XLA Modules:
  0.0 234.0 jit_solution(7603970046116702315)
XLA Ops:
  0.6 0.7 fusion.5
  1.4 0.6 pad.4.rt
  1.9 1.3 reshape.12.gain
  3.2 216.7 %shard_map.127 = (f32[64,2560]{1,0:T(8,128)}, f32[64,2560]{1,0:T(8,128)}, f32[1,2560]{1,0:T(1,128)}, bf16[768,2560]{1,0:T(8,128)(2,1)}, bf16[768,2560]{1,0:T(8,128)(2,1)}, /*index=5*/bf16[768,2560]{1,0:T(8,128)(2,1)}) custom-call(bf16[64,2560]{1,0:T(8,128)(2,1)} %bitcast.62, bf16[64,2560]{1,0:T(8,128)(2,1)} %bitcast.63, s32[8,128]{1,0:T(8,128)} %pad.4.rt, ...), custom_call_target="tpu_custom_call" | custom-call | tf_op jit(solution)/shard_map/pallas_call | solution.py:871
  220.0 1.3 reduce
  221.3 2.0 copy.60
  223.3 0.0 copy-start.1
  223.3 4.4 %copy.61 = bf16[1,768,2560]{2,1,0:T(8,128)(2,1)} copy(bf16[1,768,2560]{2,1,0:T(8,128)(2,1)} %bitcast.59) | data formatting | bytes 7864320
  227.7 0.0 copy-done.1
  227.7 0.0 copy-start
  227.7 2.0 copy.62
  229.7 1.5 copy-done
  231.2 0.0 copy-start.2
  231.2 1.9 copy.63
  233.2 0.0 copy-done.2
  233.2 0.8 copy.64
Async XLA Ops:
  223.3 4.4 %copy-start.1 = (bf16[768,2560]{1,0:T(8,128)(2,1)S(1)}, bf16[768,2560]{1,0:T(8,128)(2,1)}, u32[]{:S(2)}) copy-start(bf16[768,2560]{1,0:T(8,128)(2,1)} %get-tuple-element.14) | copy-start | bytes 11796484
  227.7 3.5 %copy-start = (bf16[768,2560]{1,0:T(8,128)(2,1)S(1)}, bf16[768,2560]{1,0:T(8,128)(2,1)}, u32[]{:S(2)}) copy-start(bf16[768,2560]{1,0:T(8,128)(2,1)} %get-tuple-element.15) | copy-start | bytes 11796484
  231.2 1.9 copy-start.2

commit v4 on v3

--- a/solution.py
+++ b/solution.py
@@ -9,7 +9,7 @@
 F32 = jnp.float32
 BF16 = jnp.bfloat16
 D = 2560
-NC = 4
+NC = 5
 CW = D // NC
 TOK = 64
 MOST = 9
@@ -44,7 +44,7 @@
     tok, dy, rt, gain, rw_in, wg_in, wu_in, wd_in,
     gx_out, gr_out, gn_out, gg_out, gu_out, gd_out,
     xall, rall, send, wg, wu, wd, acc1, acc2, q, s, h, da, db, pk,
-    rts, zt, slots, gs, gr, ds_, dr, dgt, dgr, gwrow, dgrow, rowg, dzs, gaccum, zr, row_s, rows8, cols8, rrow,
+    rts, zt, slots, gs, gr, ds_, dr, dgt, dzt, dgr, gwrow, dgrow, rowg, dzs, gaccum, zr, row_s, rows8, cols8, rrow,
     wsem, osem, lsem,
     rt_ss, rt_rs, a_ss, a_rs, b_ss, b_rs, f_ss, f_rs, d_ss, d_rs, g_ss, g_rs, dg_ss, dg_rs, dt_ss, dt_rs,
     r_ss, r_rs, z_ss, z_rs, x_ss, x_rs, zb_ss, zb_rs, zs_ss, zs_rs, p1_ss, p1_rs, p2_ss, p2_rs, p3_ss, p3_rs, free_sem,
@@ -550,7 +550,7 @@
             out_copy(i, c).start()
         return 0
 
-    ret_body(0, 0)
+    lax.fori_loop(0, 2, ret_body, 0)
 
     def dt_copy(i):
         p = (me + i) % SRC
@@ -574,7 +574,13 @@
     for i in range(1, SRC):
         dt_copy(i).start()
 
-    ret_body(1, 0)
+    lax.fori_loop(2, NC, ret_body, 0)
+
+    for b in range(8):
+        lanes = slice(b * 128, (b + 1) * 128)
+        da[lanes, 0:KA] = jnp.transpose(pk[0:KA, lanes])
+        db[lanes, 0:KB] = jnp.transpose(pk[KA:ROWS, lanes])
+
 
     for i in range(1, SRC):
         dt_copy(i).wait_recv()
@@ -597,19 +603,13 @@
     def zb_copy(i):
         t = (tsg + i) % 8
         return remote(
-            dzs.at[pl.ds(pl.multiple_of(t * 8, 8), 8)], dgt.at[myb], zb_ss.at[i - 1], zb_rs.at[i - 1], at_tsg(t)
+            dzs.at[pl.ds(pl.multiple_of(t * 8, 8), 8)], dzt.at[myb], zb_ss.at[i - 1], zb_rs.at[i - 1], at_tsg(t)
         )
 
-    for i in range(1, SRC):
-        dt_copy(i).wait_send()
-    dgt[myb] = dzs[pl.ds(pl.multiple_of(tsg * 8, 8), 8), :]
-    for i in range(1, 8):
-        pl.semaphore_signal(free_sem.at[1], inc=1, device_id=at_tsg((tsg + i) % 8), device_id_type=MESH)
-    pl.semaphore_wait(free_sem.at[1], 7)
+    dzt[myb] = dzs[pl.ds(pl.multiple_of(tsg * 8, 8), 8), :]
     for i in range(1, 8):
         zb_copy(i).start()
 
-    lax.fori_loop(2, NC - 1, ret_body, 0)
 
     def zs_copy(d):
         return remote(gs.at[d], zr.at[seat], zs_ss.at[d], zs_rs.at[seat], at_dest(d))
@@ -617,20 +617,15 @@
     def zs_arrival(e):
         return remote(gs.at[e], zr.at[e], zs_ss.at[e], zs_rs.at[e], at_src(e))
 
-    for i in range(1, 8):
-        zb_copy(i).wait_recv()
-    others(own_d, lambda d: g_copy(d).wait_send())
-    for b in range(8):
-        rows8[:, b * 128 : (b + 1) * 128] = dgt[b]
-    to_slots()
-    zr[seat] = gs[own_d]
-    others(own_d, lambda d: zs_copy(d).start())
-    ret_body(NC - 1, 0)
-
-    for b in range(8):
-        lanes = slice(b * 128, (b + 1) * 128)
-        da[lanes, 0:KA] = jnp.transpose(pk[0:KA, lanes])
-        db[lanes, 0:KB] = jnp.transpose(pk[KA:ROWS, lanes])
+    def slots_out():
+        for i in range(1, 8):
+            zb_copy(i).wait_recv()
+        others(own_d, lambda d: g_copy(d).wait_send())
+        for b in range(8):
+            rows8[:, b * 128 : (b + 1) * 128] = dzt[b]
+        to_slots()
+        zr[seat] = gs[own_d]
+        others(own_d, lambda d: zs_copy(d).start())
 
     def p1_rows(d):
         return acc2.at[pl.ds(pl.multiple_of(d * 48, 8), 48), pl.ds(0, 128)]
@@ -783,29 +778,37 @@
             for i in (1, 3, 2):
                 x_copy(c, i, False).start()
 
+    def own_router():
+        pad = jnp.concatenate([dzs[...], jnp.zeros((64, 128), F32)], axis=0)
+        acc1[0:128, 0:128] = jnp.transpose(pad)
+        dz_own = acc1[pl.ds(pl.multiple_of(dp * TOK, TOK), TOK), 0:EXPERTS]
+        hi, lo = split(dz_own)
+        both = dot(jnp.concatenate([hi, lo], axis=0), order()).astype(BF16)
+        for c in range(NC):
+            cols = slice(c * CW, (c + 1) * CW)
+            two = dot(both, rw_in[:, cols])
+            gx_out[:, cols] = two[0:TOK] + two[TOK : 2 * TOK]
+
+    wgrad_body(0, 0)
     comb_body(0)
-    wgrad_body(0, 0)
+    slots_out()
+    wgrad_body(1, 0)
     comb_body(1)
     z_sum(0)
-    lax.fori_loop(1, 3, wgrad_body, 0)
+    wgrad_body(2, 0)
     comb_body(2)
     z_sum(1)
     wgrad_body(3, 0)
-    router_row()
     comb_body(3)
     z_sum(2)
+    wgrad_body(4, 0)
+    router_row()
+    comb_body(4)
+    z_sum(3)
     router_rows()
-    z_sum(3)
-
-    pad = jnp.concatenate([dzs[...], jnp.zeros((64, 128), F32)], axis=0)
-    acc1[0:128, 0:128] = jnp.transpose(pad)
-    dz_own = acc1[pl.ds(pl.multiple_of(dp * TOK, TOK), TOK), 0:EXPERTS]
-    hi, lo = split(dz_own)
-    both = dot(jnp.concatenate([hi, lo], axis=0), order()).astype(BF16)
-    for c in range(NC):
-        cols = slice(c * CW, (c + 1) * CW)
-        two = dot(both, rw_in[:, cols])
-        gx_out[:, cols] = two[0:TOK] + two[TOK : 2 * TOK]
+    own_router()
+    z_sum(4)
+
     wide = tok[...].astype(F32)
     inv = lax.rsqrt(jnp.mean(wide * wide, axis=1, keepdims=True) + 1e-06)
 
@@ -860,6 +863,7 @@
     others(seat, lambda e: p1_copy(e).wait_send())
     for i in range(1, SRC):
         p3_copy(i).wait_send()
+        dt_copy(i).wait_send()
 
 
 def call(tok, dy, rt, gain, rwt, wg, wu, wd):
@@ -892,7 +896,7 @@
             V((16, ALL), jnp.int32),
             V((8, 8, 256), F32), V((8, 8, 256), F32),
             V((8, 8, 256), F32), V((8, 8, 256), F32),
-            V((8, 8, 128), F32), V((SRC, 8, 128), F32),
+            V((8, 8, 128), F32), V((8, 8, 128), F32), V((SRC, 8, 128), F32),
             V((8, ROWS), F32), V((8, ROWS), F32),
             V((1, ALL), F32), V((EXPERTS, 128), F32),
             V((NC, 8, CW), F32), V((8, 8, 256), F32), V((48, 128), F32), V((8, ALL), F32), V((256, 128), F32), V((NC, 8, CW), F32),
@@ -906,7 +910,7 @@
             S((NC, 3)), S((NC, 3)), S((NC, 3)), S((NC, 3)),
             S((7,)), S((7,)), S((8,)), S((8,)), S((8,)), S((8,)),
             S((7,)), S((7,)), S((15,)), S((15,)),
-            pltpu.SemaphoreType.REGULAR((2,)),
+            pltpu.SemaphoreType.REGULAR((1,)),
         ],
         compiler_params=pltpu.CompilerParams(
             collective_id=0, has_side_effects=True, vmem_limit_bytes=VMEM_LIMIT

time: 235 us -> 229 us (0.974)
  Pallas kernels: 217 us -> 212 us
    pallas_call x1, Pallas kernels: 217 us -> 212 us  [call(): pl.pallas_call(kernel, out_shape=(jax.ShapeDtypeStruct((TOK, D), F32), ja...]
where the time goes in v4:
time: 229 us
  Pallas kernels  212 us (93%)
  local copies, waits for them, and re-layouts  14.6 us (6%)
    pallas_call x1, Pallas kernels, call(): pl.pallas_call(kernel, out_shape=(jax.ShapeDtypeStruct((TOK, D), F32), ja...  212 us
    unnamed x11, local copies, waits for them, and re-layouts  12.7 us

profile of v4, /device:TPU:1, one launch (start us, length us, event | category | flops | bytes accessed | tf_op | source)
XLA Modules:
  0.0 228.9 jit_solution(1399438012839971351)
XLA Ops:
  0.6 0.7 fusion.5
  1.4 0.6 pad.4.rt
  1.9 1.3 reshape.12.gain
  3.2 211.6 %shard_map.127 = (f32[64,2560]{1,0:T(8,128)}, f32[64,2560]{1,0:T(8,128)}, f32[1,2560]{1,0:T(1,128)}, bf16[768,2560]{1,0:T(8,128)(2,1)}, bf16[768,2560]{1,0:T(8,128)(2,1)}, /*index=5*/bf16[768,2560]{1,0:T(8,128)(2,1)}) custom-call(bf16[64,2560]{1,0:T(8,128)(2,1)} %bitcast.62, bf16[64,2560]{1,0:T(8,128)(2,1)} %bitcast.63, s32[8,128]{1,0:T(8,128)} %pad.4.rt, ...), custom_call_target="tpu_custom_call" | custom-call | tf_op jit(solution)/shard_map/pallas_call | solution.py:875
  214.9 1.3 reduce
  216.2 2.0 copy.60
  218.2 0.0 copy-start.1
  218.2 4.4 %copy.61 = bf16[1,768,2560]{2,1,0:T(8,128)(2,1)} copy(bf16[1,768,2560]{2,1,0:T(8,128)(2,1)} %bitcast.59) | data formatting | bytes 7864320
  222.6 0.0 copy-done.1
  222.6 0.0 copy-start
  222.6 2.0 copy.62
  224.6 1.5 copy-done
  226.1 0.0 copy-start.2
  226.1 1.9 copy.63
  228.1 0.0 copy-done.2
  228.1 0.8 copy.64
Async XLA Ops:
  218.2 4.4 %copy-start.1 = (bf16[768,2560]{1,0:T(8,128)(2,1)S(1)}, bf16[768,2560]{1,0:T(8,128)(2,1)}, u32[]{:S(2)}) copy-start(bf16[768,2560]{1,0:T(8,128)(2,1)} %get-tuple-element.14) | copy-start | bytes 11796484
  222.6 3.5 %copy-start = (bf16[768,2560]{1,0:T(8,128)(2,1)S(1)}, bf16[768,2560]{1,0:T(8,128)(2,1)}, u32[]{:S(2)}) copy-start(bf16[768,2560]{1,0:T(8,128)(2,1)} %get-tuple-element.15) | copy-start | bytes 11796484
  226.1 1.9 copy-start.2
